TPU v7x, 32 devices: a whole 2x2x4 slice. The times are simulated.
32 devices in a mesh: groups: 2 (over x), region: 16 (over z, y, core).
Axes of the slice: x: 2, y: 2, z: 4, core: 2. Of those that a mesh axis runs over, the one named last changes fastest.
Arguments:
- tangent: float32 [4096, 10, 128], P(('groups', 'region')), parts along dimension 0, may hold values from -6 to 6
- transport: bfloat16 [2, 2048, 4, 128, 128], P(None, 'region'), may hold values from -0.25 to 0.25
- block_column: int32 [2, 2048, 4], P(None, 'region'), may hold values from 0 to 2047, as said below
- cell_order: int32 [32, 64], P(None, 'region'), may hold values from 0 to 2047, as said below
- depths: int32 [8192], P('region'), may hold values from 1 to 32, as said below
- rates: float32 [32, 8192], P(None, 'region'), may hold values from 0.1 to 1
- coupling: float32 [10, 10], replicated, may hold values from -2 to 2
- sinking: float32 [10], replicated, may hold values from 0.05 to 0.9
Outputs:
- advanced: float32 [4096, 10, 128], P(('groups', 'region')), parts along dimension 0
There are 2 independent parts, one for each index of `groups`. A program takes and returns all parts, laid end to end along the dimension named above; an argument that names none is the same for every part. Nothing has to cross between parts.
Inputs may be any that keep to these rules, and one draw needn't show every extreme that they name: block_column[s, t, b] names a tile held by the region device of tile t or one of its two neighbours, with wrap around. cell_order is a permutation of all tiles; the column blocks of a region device use exactly that device's tiles. `depths`: each region device holds a column of depth 32.
All inputs are finite; a program needn't handle non-finite values.
Results may differ from a plain program's by a relative error of at most 0.0003.
Values sent between devices are 32-bit elements; how exact they have to be, the bound alone decides.
No kernel may reach another device: no remote copies, remote signals or barrier semaphores. Data moves between devices by JAX's collectives and lax.ppermute only.
A program may use at most 128 MiB of HBM per device.

v0:
```python
import jax
import jax.numpy as jnp
from jax import lax
from jax.sharding import PartitionSpec as P


def padded(shard, sides, width):
    for axis, dim in sides:
        size, length = (lax.axis_size(axis), shard.shape[dim])
        up = [(i, (i + 1) % size) for i in range(size)]
        down = [(j, i) for i, j in up]
        last = lax.slice_in_dim(shard, length - width, length, axis=dim)
        first = lax.slice_in_dim(shard, 0, width, axis=dim)
        before = lax.ppermute(last, axis, up)
        after = lax.ppermute(first, axis, down)
        shard = jnp.concatenate([before, shard, after], axis=dim)
    return shard


def column_chain(cols, rates, depths, coupling, sinking):
    levels = cols.shape[0]
    level_ids = jnp.arange(levels, dtype=jnp.int32)

    def advance(carry, inputs):
        values, rate_row, level = inputs
        mixed = jnp.einsum(
            "rs,bsw->brw",
            coupling,
            values,
            precision=lax.Precision.HIGHEST,
            preferred_element_type=jnp.float32,
        )
        result = values + rate_row[:, None, :] * mixed + carry
        result = jnp.where((level < depths)[:, None, :], result, jnp.float32(0.0))
        return (sinking[None, :, None] * result, result)

    start = jnp.zeros(cols.shape[1:], jnp.float32)
    final, outputs = lax.scan(advance, start, (cols, rates, level_ids))
    return outputs


def transport_step(field, blocks, picks):
    tile_dev = field.shape[0]
    regions = lax.axis_size("region")
    here = lax.axis_index("region")
    extended = padded(field, (("region", 0),), tile_dev)
    slot_of = (picks // tile_dev - here + 1) % regions * tile_dev + picks % tile_dev
    picked = extended[slot_of]
    return jnp.einsum(
        "tbij,tbrj->tri",
        blocks,
        picked,
        precision=lax.Precision.HIGHEST,
        preferred_element_type=jnp.float32,
    )


def shards(tangent, transport, block_column, cell_order, depths, rates, coupling, sinking):
    field = tangent
    for step in range(2):
        field = transport_step(field, transport[step], block_column[step])
    tile_dev = field.shape[0]
    tracers = field.shape[1]
    levels = cell_order.shape[0]
    col_blocks = cell_order.shape[1]
    here = lax.axis_index("region")
    local_tiles = cell_order - here * tile_dev
    cols = field[local_tiles]
    rate_rows = rates.reshape(levels, col_blocks, 128)
    depth_rows = depths.reshape(col_blocks, 128)
    result = column_chain(cols, rate_rows, depth_rows, coupling, sinking)
    back = jnp.zeros((tile_dev, tracers, 128), jnp.float32)
    return back.at[local_tiles.reshape(-1)].set(result.reshape(levels * col_blocks, tracers, 128))


def solution(mesh):
    in_specs = (
        P(("groups", "region"), None, None),
        P(None, "region", None, None, None),
        P(None, "region", None),
        P(None, "region"),
        P("region"),
        P(None, "region"),
        P(),
        P(),
    )
    out_specs = P(("groups", "region"), None, None)
    return jax.shard_map(shards, mesh=mesh, in_specs=in_specs, out_specs=out_specs, check_vma=False)
```

profile of v0, /device:TPU:1, one launch (start us, length us, event | category | flops | bytes accessed | tf_op | source)
XLA Modules:
  0.0 130.6 jit_solution(9436496581755162399)
XLA Ops:
  0.0 2.6 %collective-permute-start = (f32[128,10,128]{2,0,1:T(8,128)}, f32[128,10,128]{2,0,1:T(8,128)S(1)}, u32[]{:S(2)}, u32[]{:S(2)}) collective-permute-start(f32[128,10,128]{2,0,1:T(8,128)} %param.10), channel_id=1, source_target_pairs={{0,1},{1,2},{2,3},{3,4},{4,5},{5,6},{6,7},{7,8},{8,9},{9,10},{10,1... | collective-permute-start | bytes 1966088 | tf_op jit(solution)/shard_map/ppermute | solution.py:14
  2.6 2.5 %copy.23 = f32[128,10,128]{2,1,0:T(8,128)} copy(f32[128,10,128]{2,0,1:T(8,128)} %param.10) | data formatting | bytes 1310720 | tf_op args[0]
  5.1 0.7 compare_select_fusion.1
  6.3 11.2 %collective-permute-done = f32[128,10,128]{2,0,1:T(8,128)S(1)} collective-permute-done((f32[128,10,128]{2,0,1:T(8,128)}, f32[128,10,128]{2,0,1:T(8,128)S(1)}, u32[]{:S(2)}, u32[]{:S(2)}) %collective-permute-start) | collective-permute-done | bytes 655392 | tf_op jit(solution)/shard_map/ppermute | solution.py:14
  17.9 2.0 %collective-permute-done.1 = f32[128,10,128]{2,0,1:T(8,128)S(1)} collective-permute-done((f32[128,10,128]{2,0,1:T(8,128)}, f32[128,10,128]{2,0,1:T(8,128)S(1)}, u32[]{:S(2)}, u32[]{:S(2)}) %collective-permute-start.1) | collective-permute-done | bytes 655392 | tf_op jit(solution)/shard_map/ppermute | solution.py:15
  20.3 1.4 %pad_maximum_fusion = f32[384,10,128]{2,1,0:T(8,128)S(1)} fusion(f32[128,10,128]{2,1,0:T(8,128)S(1)} %copy.24, f32[128,10,128]{2,1,0:T(8,128)} %copy.23, f32[128,10,128]{2,1,0:T(8,128)S(1)} %copy.22), kind=kLoop, calls=%fused_computation.23 | loop fusion | flops 983040 | bytes 3932160 | tf_op jit(solution)/shard_map/concatenate | solution.py:16
  21.7 3.1 %gather_fusion = f32[512,10,128]{2,1,0:T(8,128)} fusion(f32[384,10,128]{2,1,0:T(8,128)S(1)} %pad_maximum_fusion, s32[1024]{0:T(1024)S(1)} %pad_clamp_fusion.2), kind=kCustom, calls=%fused_computation | custom fusion | bytes 5244928 | tf_op jit(solution)/shard_map/gather | solution.py:48
  24.8 16.5 %fusion.14 = f32[128,10,128]{2,1,0:T(8,128)S(1)} fusion(f32[128,4,10,128]{3,2,1,0:T(8,128)} %bitcast.98, bf16[2,128,4,128,128]{4,3,2,1,0:T(8,128)(2,1)} %param.11), kind=kOutput, calls=%fused_computation.25 | convolution fusion | flops 1006632960 | bytes 21626880 | tf_op jit(solution)/shard_map/tbij,tbrj->tri/dot_general | solution.py:49
  41.3 1.0 copy-done
  43.6 14.0 %collective-permute-done.2 = f32[128,10,128]{2,0,1:T(8,128)S(1)} collective-permute-done((f32[128,10,128]{2,0,1:T(8,128)S(1)}, f32[128,10,128]{2,0,1:T(8,128)S(1)}, u32[]{:S(2)}, u32[]{:S(2)}) %collective-permute-start.2) | collective-permute-done | bytes 655392 | tf_op jit(solution)/shard_map/ppermute | solution.py:14
  58.4 1.4 %pad_maximum_fusion.1 = f32[384,10,128]{2,1,0:T(8,128)S(1)} fusion(f32[128,10,128]{2,1,0:T(8,128)S(1)} %copy.29, f32[128,10,128]{2,1,0:T(8,128)} %copy-done, f32[128,10,128]{2,1,0:T(8,128)S(1)} %copy.28), kind=kLoop, calls=%fused_computation.24 | loop fusion | flops 983040 | bytes 3932160 | tf_op jit(solution)/shard_map/concatenate | solution.py:16
  59.8 3.1 %gather_fusion.1 = f32[512,10,128]{2,1,0:T(8,128)} fusion(f32[384,10,128]{2,1,0:T(8,128)S(1)} %pad_maximum_fusion.1, s32[1024]{0:T(1024)S(1)} %pad_clamp_fusion.1), kind=kCustom, calls=%fused_computation.1 | custom fusion | bytes 5244928 | tf_op jit(solution)/shard_map/gather | solution.py:48
  62.9 16.6 %fusion.17 = f32[128,10,128]{2,1,0:T(8,128)S(1)} fusion(f32[128,4,10,128]{3,2,1,0:T(8,128)} %bitcast.99, bf16[2,128,4,128,128]{4,3,2,1,0:T(8,128)(2,1)} %param.11), kind=kOutput, calls=%fused_computation.26 | convolution fusion | flops 1006632960 | bytes 21626880 | tf_op jit(solution)/shard_map/tbij,tbrj->tri/dot_general | solution.py:49
  79.5 0.8 gather_fusion.2
  80.3 44.9 %while.13 = (s32[]{:T(128)}, f32[4,10,128]{2,1,0:T(8,128)S(1)}, f32[32,4,10,128]{3,2,1,0:T(8,128)S(1)}, f32[10]{0:T(128)S(1)}, s32[32]{0:T(128)S(1)}, /*index=5*...) while((s32[]{:T(128)}, f32[4,10,128]{2,1,0:T(8,128)S(1)}, ...), condition=%wide.region_1.2_spmd.clone, body=%wide.region_0.1_spmd.clone.sunk | while | flops 645635 | bytes 223887 | solution.py:38
  80.3 0.6 dynamic_slice.27
  81.7 0.6 dynamic_slice.27
  83.1 0.6 dynamic_slice.27
  84.5 0.6 dynamic_slice.27
  85.9 0.6 dynamic_slice.27
  87.3 0.6 dynamic_slice.27
  88.7 0.6 dynamic_slice.27
  90.1 0.6 dynamic_slice.27
  91.5 0.6 dynamic_slice.27
  92.9 0.6 dynamic_slice.27
  94.3 0.6 dynamic_slice.27
  95.7 0.6 dynamic_slice.27
  97.1 0.6 dynamic_slice.27
  98.5 0.6 dynamic_slice.27
  99.9 0.6 dynamic_slice.27
  101.3 0.6 dynamic_slice.27
  102.7 0.6 dynamic_slice.27
  104.1 0.6 dynamic_slice.27
  105.5 0.6 dynamic_slice.27
  106.9 0.6 dynamic_slice.27
  108.3 0.6 dynamic_slice.27
  109.7 0.6 dynamic_slice.27
  111.1 0.6 dynamic_slice.27
  112.5 0.6 dynamic_slice.27
  115.3 0.6 dynamic_slice.27
  116.7 0.6 dynamic_slice.27
  118.1 0.6 dynamic_slice.27
  119.5 0.6 dynamic_slice.27
  121.0 0.6 dynamic_slice.27
  122.4 0.6 dynamic_slice.27
  123.8 0.6 dynamic_slice.27
  125.2 4.3 %scatter_fusion = f32[128,10,128]{2,1,0:T(8,128)S(1)} fusion(f32[128,10,128]{2,1,0:T(8,128)S(1)} %broadcast_in_dim.34, s32[128]{0:T(128)S(1)} %fusion.34, f32[128,10,128]{2,1,0:T(8,128)S(1)} %bitcast.101), kind=kCustom, calls=%fused_computation.3 | custom fusion | bytes 1966592 | tf_op jit(solution)/shard_map/scatter | solution.py:73
  129.6 1.0 copy.32
  (169 shorter events, 28.4 us)
Async XLA Ops:
  0.0 17.5 %collective-permute-start = (f32[128,10,128]{2,0,1:T(8,128)}, f32[128,10,128]{2,0,1:T(8,128)S(1)}, u32[]{:S(2)}, u32[]{:S(2)}) collective-permute-start(f32[128,10,128]{2,0,1:T(8,128)} %param.10), channel_id=1, source_target_pairs={{0,1},{1,2},{2,3},{3,4},{4,5},{5,6},{6,7},{7,8},{8,9},{9,10},{10,1... | collective-permute-start | bytes 1966088 | tf_op jit(solution)/shard_map/ppermute | solution.py:14
  2.6 17.2 %collective-permute-start.1 = (f32[128,10,128]{2,0,1:T(8,128)}, f32[128,10,128]{2,0,1:T(8,128)S(1)}, u32[]{:S(2)}, u32[]{:S(2)}) collective-permute-start(f32[128,10,128]{2,0,1:T(8,128)} %param.10), channel_id=1, source_target_pairs={{1,0},{2,1},{3,2},{4,3},{5,4},{6,5},{7,6},{8,7},{9,8},{10,9},{11,1... | collective-permute-start | bytes 1966088 | tf_op jit(solution)/shard_map/ppermute | solution.py:15
  24.8 18.3 %copy-start.6 = (s32[32,4]{0,1:T(4,128)S(1)}, s32[32,4]{0,1:T(4,128)}, u32[]{:S(2)}) copy-start(s32[32,4]{0,1:T(4,128)} %param.13) | copy-start | bytes 1540
  24.8 18.5 %copy-start.3 = (f32[32,512]{1,0:T(8,128)S(1)}, f32[32,512]{1,0:T(8,128)}, u32[]{:S(2)}) copy-start(f32[32,512]{1,0:T(8,128)} %param.15) | copy-start | bytes 196612
  41.3 1.0 copy-start
  42.5 15.0 %collective-permute-start.2 = (f32[128,10,128]{2,0,1:T(8,128)S(1)}, f32[128,10,128]{2,0,1:T(8,128)S(1)}, u32[]{:S(2)}, u32[]{:S(2)}) collective-permute-start(f32[128,10,128]{2,0,1:T(8,128)S(1)} %copy.26), channel_id=1, source_target_pairs={{0,1},{1,2},{2,3},{3,4},{4,5},{5,6},{6,7},{7,8},{8,9},{9,10},{10,1... | collective-permute-start | bytes 1966088 | tf_op jit(solution)/shard_map/ppermute | solution.py:14
  43.0 15.0 %collective-permute-start.3 = (f32[128,10,128]{2,0,1:T(8,128)S(1)}, f32[128,10,128]{2,0,1:T(8,128)S(1)}, u32[]{:S(2)}, u32[]{:S(2)}) collective-permute-start(f32[128,10,128]{2,0,1:T(8,128)S(1)} %copy.26), channel_id=1, source_target_pairs={{1,0},{2,1},{3,2},{4,3},{5,4},{6,5},{7,6},{8,7},{9,8},{10,9},{11,1... | collective-permute-start | bytes 1966088 | tf_op jit(solution)/shard_map/ppermute | solution.py:15
  62.9 17.4 %copy-start.1 = (f32[32,4,10,128]{3,2,1,0:T(8,128)S(1)}, f32[32,4,10,128]{3,2,1,0:T(8,128)}, u32[]{:S(2)}) copy-start(f32[32,4,10,128]{3,2,1,0:T(8,128)} %custom-call.7) | copy-start | bytes 1966084
  62.9 17.4 %copy-start.2 = (f32[10,10]{1,0:T(8,128)S(1)}, f32[10,10]{1,0:T(8,128)}, u32[]{:S(2)}) copy-start(f32[10,10]{1,0:T(8,128)} %param.16) | copy-start | bytes 1204
  62.9 17.4 %copy-start.4 = (s32[512]{0:T(512)S(1)}, s32[512]{0:T(512)}, u32[]{:S(2)}) copy-start(s32[512]{0:T(512)} %param.14) | copy-start | bytes 6148
  62.9 17.4 %copy-start.5 = (f32[10]{0:T(128)S(1)}, f32[10]{0:T(128)}, u32[]{:S(2)}) copy-start(f32[10]{0:T(128)} %param.17) | copy-start | bytes 124
where the time goes:
time: 131 us
  matrix products  38.8 us (30%)
  local copies, waits for them, and re-layouts  38 us (29%)
  waiting for transfers between devices  27.1 us (21%)
  other arithmetic  21.7 us (17%)
  starting transfers between devices  3.19 us (2%)
  loops' own time  1.62 us (1%)
    dot_general x2, matrix products, transport_step(): jnp.einsum('tbij,tbrj->tri', blocks, picked, precision=lax.Precision.HIGH...  33.1 us
    ppermute x2, waiting for transfers between devices, padded(): before = lax.ppermute(last, axis, up)  25.2 us
    dynamic_slice x32, local copies, waits for them, and re-layouts, column_chain(): final, outputs = lax.scan(advance, start, (cols, rates, level_ids))  18.8 us
    lt x32, other arithmetic, advance(): result = jnp.where((level < depths)[:, None, :], result, jnp.float32(0.0))  18.1 us
    gather x2, local copies, waits for them, and re-layouts, transport_step(): picked = extended[slot_of]  6.15 us
    dot_general x32, matrix products, advance(): jnp.einsum('rs,bsw->brw', coupling, values, precision=lax.Precision.HIGHE...  5.71 us
    scatter x2, local copies, waits for them, and re-layouts, shards(): back.at[local_tiles.reshape(-1)]  5.37 us
    unnamed x15, local copies, waits for them, and re-layouts  3.48 us
  transfers between devices with their start and end apart: 4, of which 3 were waited for; matrix products, arithmetic and copies ran while one was open for 4% of the time, Pallas kernels for 0%

commit v1 on v0

v1 whole, which is shorter than its diff:
```python
import functools

import jax
import jax.numpy as jnp
from jax import lax
from jax.experimental import pallas as pl
from jax.experimental.pallas import tpu as pltpu
from jax.sharding import PartitionSpec as P

GROUP = 8
ROWS = 16
VMEM_LIMIT = 48 * 1024 * 1024


def split_rows(field, row, tiles):
    x = field[pl.ds(row, ROWS, stride=tiles), :]
    high = x.astype(jnp.bfloat16)
    low = (x - high.astype(jnp.float32)).astype(jnp.bfloat16)
    return jnp.concatenate([high, low], axis=0)


def tile_product(slots, field, blocks, t, tile, tiles, nb):
    xs = [split_rows(field, slots[b, t], tiles) for b in range(nb)]
    ts = [blocks[tile, b] for b in range(nb)]
    acc = lax.dot_general(
        jnp.concatenate(xs, axis=1),
        jnp.concatenate(ts, axis=1),
        (((1,), (1,)), ((), ())),
        preferred_element_type=jnp.float32,
    )
    return acc[:ROWS] + acc[ROWS:]


def load_field(own, near, far, field, sem):
    rows = own.shape[0]
    copies = [
        pltpu.make_async_copy(ref, field.at[pl.ds(i * rows, rows)], sem.at[i])
        for i, ref in enumerate((own, near, far))
    ]
    for copy in copies:
        copy.start()
    return copies


def first_kernel(tiles, nb, ntr, slots, own, near, far, transport, out, field, blocks, fsem, bsem):
    copies = load_field(own, near, far, field, fsem)
    chunks = tiles // GROUP

    def block_copy(c):
        at = pl.ds(c * GROUP, GROUP)
        return pltpu.make_async_copy(transport.at[0, at], blocks.at[at], bsem.at[c])

    for c in range(chunks):
        block_copy(c).start()
    for copy in copies:
        copy.wait()

    def step(c, _):
        block_copy(c).wait()
        for u in range(GROUP):
            t = c * GROUP + u
            v = tile_product(slots, field, blocks, t, t, tiles, nb)
            out[pl.ds(t, ntr, stride=tiles), :] = v[:ntr]
        return 0

    lax.fori_loop(0, chunks, step, 0)


def second_kernel(tiles, nb, ntr, levels, slots, order, own, near, far, rates, depths, mix, sink, transport, out,
                  field, blocks, value, fsem, bsem):
    copies = load_field(own, near, far, field, fsem)
    col_blocks = tiles // levels
    per = GROUP // col_blocks
    steps = tiles // GROUP

    def block_copy(n):
        return pltpu.make_async_copy(transport.at[1, order[n]], blocks.at[n], bsem.at[n])

    ahead = 4

    def start_group(c):
        for u in range(GROUP):
            block_copy(c * GROUP + u).start()

    for c in range(ahead):
        start_group(c)
    for copy in copies:
        copy.wait()

    def products(c):
        for u in range(GROUP):
            block_copy(c * GROUP + u).wait()
        for u in range(GROUP):
            n = c * GROUP + u
            value[lax.rem(c, 2), u] = tile_product(slots, field, blocks, order[n], n, tiles, nb)

    def chain(c, carry):
        carry = list(carry)
        for l in range(per):
            k = c * per + l
            for q in range(col_blocks):
                u = l * col_blocks + q
                v = value[lax.rem(c, 2), u]
                mixed = mix[0] * v[0:1]
                for s in range(1, ntr):
                    mixed = mixed + mix[s] * v[s:s + 1]
                cells = slice(q * 128, (q + 1) * 128)
                rate = rates[k, q:q + 1]
                wet = k < depths[:, cells]
                y = jnp.where(wet, v + rate * mixed + carry[q], jnp.float32(0.0))
                carry[q] = sink[...] * y
                out[pl.ds(order[c * GROUP + u], ntr, stride=tiles), :] = y[:ntr]
        return tuple(carry)

    products(0)

    def step(c, carry):
        @pl.when(c + ahead - 1 < steps)
        def _():
            start_group(c + ahead - 1)

        products(c)
        return chain(c - 1, carry)

    carry = tuple(jnp.zeros((ROWS, 128), jnp.float32) for _ in range(col_blocks))
    carry = lax.fori_loop(1, steps, step, carry)
    chain(steps - 1, carry)


def exchange(rows):
    n = lax.axis_size("region")
    near = [(i, i ^ 1) for i in range(n)]
    far = [(i, (i + 1) % n if i % 2 else (i - 1) % n) for i in range(n)]
    b = lax.ppermute(rows, "region", far)
    a = lax.ppermute(rows, "region", near)
    return a, b


def shards(tangent, transport, block_column, cell_order, depths, rates, coupling, sinking):
    tiles, ntr, cells = tangent.shape
    nb = block_column.shape[2]
    levels = cell_order.shape[0]
    rows = ntr * tiles
    here = lax.axis_index("region")
    planar = jnp.transpose(tangent, (1, 0, 2)).reshape(rows, cells)
    near, far = exchange(planar)

    picks = jnp.transpose(block_column, (0, 2, 1))
    home = picks // tiles
    place = jnp.where(home == here, 0, jnp.where(home == (here ^ 1), 1, 2))
    slots = place * rows + picks % tiles
    order = (cell_order - here * tiles).reshape(-1)
    mix = jnp.pad(coupling.T, ((0, 0), (0, ROWS - ntr)))[:, :, None] * jnp.ones((1, 1, cells), jnp.float32)
    sink = jnp.pad(sinking, (0, ROWS - ntr))[:, None] * jnp.ones((1, cells), jnp.float32)

    smem = pl.BlockSpec(memory_space=pltpu.SMEM)
    vmem = pl.BlockSpec(memory_space=pltpu.VMEM)
    anyw = pl.BlockSpec(memory_space=pl.ANY)
    out_shape = jax.ShapeDtypeStruct((rows, cells), jnp.float32)
    params = pltpu.CompilerParams(vmem_limit_bytes=VMEM_LIMIT)
    field = pltpu.VMEM((3 * rows + (ROWS - ntr) * tiles, cells), jnp.float32)
    blocks = pltpu.VMEM((tiles, nb, cells, cells), jnp.bfloat16)
    flops = 2 * 2 * tiles * nb * cells * cells * ntr

    middle = pl.pallas_call(
        functools.partial(first_kernel, tiles, nb, ntr),
        out_shape=out_shape,
        in_specs=[smem, anyw, anyw, anyw, anyw],
        out_specs=vmem,
        scratch_shapes=[field, blocks, pltpu.SemaphoreType.DMA((3,)), pltpu.SemaphoreType.DMA((tiles // GROUP,))],
        compiler_params=params,
        cost_estimate=pl.CostEstimate(flops=flops, bytes_accessed=transport.size, transcendentals=0),
        name="step_one",
    )(slots[0], planar, near, far, transport)

    near, far = exchange(middle)
    result = pl.pallas_call(
        functools.partial(second_kernel, tiles, nb, ntr, levels),
        out_shape=out_shape,
        in_specs=[smem, smem, anyw, anyw, anyw, vmem, vmem, vmem, vmem, anyw],
        out_specs=vmem,
        scratch_shapes=[
            field,
            blocks,
            pltpu.VMEM((2, GROUP, ROWS, cells), jnp.float32),
            pltpu.SemaphoreType.DMA((3,)),
            pltpu.SemaphoreType.DMA((tiles,)),
        ],
        compiler_params=params,
        cost_estimate=pl.CostEstimate(flops=flops, bytes_accessed=transport.size, transcendentals=0),
        name="step_two_columns",
    )(slots[1], order, middle, near, far, rates.reshape(levels, -1, cells), depths.reshape(1, -1), mix, sink, transport)
    return jnp.transpose(result.reshape(ntr, tiles, cells), (1, 0, 2))


def solution(mesh):
    in_specs = (
        P(("groups", "region"), None, None),
        P(None, "region", None, None, None),
        P(None, "region", None),
        P(None, "region"),
        P("region"),
        P(None, "region"),
        P(),
        P(),
    )
    out_specs = P(("groups", "region"), None, None)
    return jax.shard_map(shards, mesh=mesh, in_specs=in_specs, out_specs=out_specs, check_vma=False)
```

time: 131 us -> 58.5 us (0.45)
  matrix products: 38.8 us -> 0 us
  local copies, waits for them, and re-layouts: 38 us -> 1.57 us
  Pallas kernels: 0 us -> 23.8 us
  other arithmetic: 21.7 us -> 0.71 us
  starting transfers between devices: 3.19 us -> 7.38 us
  waiting for transfers between devices: 27.1 us -> 24.8 us
  loops' own time: 1.62 us -> 0 us
    dot_general x34 -> x0, matrix products: 38.8 us -> none  [the longest x2 33.1 us: transport_step(): jnp.einsum('tbij,tbrj->tri', blocks, picked, precision=lax.Precision.HIGH...]
    pallas_call x0 -> x2, Pallas kernels: none -> 23.8 us  [the longest x1 13.6 us: shards(): pl.pallas_call(functools.partial(second_kernel, tiles, nb, ntr, levels),...]
    dynamic_slice x32 -> x0, local copies, waits for them, and re-layouts: 18.8 us -> none  [column_chain(): final, outputs = lax.scan(advance, start, (cols, rates, level_ids))]
    lt x32 -> x0, other arithmetic: 18.1 us -> none  [advance(): result = jnp.where((level < depths)[:, None, :], result, jnp.float32(0.0))]
    gather x3 -> x0, local copies, waits for them, and re-layouts: 6.9 us -> none  [the longest x2 6.15 us: transport_step(): picked = extended[slot_of]]
    scatter x2 -> x0, local copies, waits for them, and re-layouts: 5.37 us -> none  [shards(): back.at[local_tiles.reshape(-1)]]
    ppermute x4, starting transfers between devices: 3.19 us -> 7.38 us  [the longest x2 4.51 us: exchange(): b = lax.ppermute(rows, 'region', far)]
    concatenate x2 -> x0, other arithmetic: 2.86 us -> none  [padded(): shard = jnp.concatenate([before, shard, after], axis=dim)]
  transfers between devices with their start and end apart: 4 -> 4, of which waited for: 3 -> 2; matrix products, arithmetic and copies ran while one was open for 4% -> 2% of each run, Pallas kernels for 0% -> 0%
where the time goes in v1:
time: 58.5 us; the launch traced here: 58.4 us
  waiting for transfers between devices  24.8 us (42%)
  Pallas kernels  23.8 us (41%)
  starting transfers between devices  7.38 us (13%)
  local copies, waits for them, and re-layouts  1.57 us (3%)
  other arithmetic  0.71 us (1%)
    ppermute x2, waiting for transfers between devices, exchange(): b = lax.ppermute(rows, 'region', far)  24.8 us
    pallas_call x1, Pallas kernels, shards(): pl.pallas_call(functools.partial(second_kernel, tiles, nb, ntr, levels),...  13.6 us
    pallas_call x1, Pallas kernels, shards(): pl.pallas_call(functools.partial(first_kernel, tiles, nb, ntr), out_shape...  10.2 us
    ppermute x2, starting transfers between devices, exchange(): b = lax.ppermute(rows, 'region', far)  4.51 us
    ppermute x2, starting transfers between devices, exchange(): a = lax.ppermute(rows, 'region', near)  2.87 us
    unnamed x13, local copies, waits for them, and re-layouts  1.2 us
  transfers between devices with their start and end apart: 4, of which 2 were waited for; matrix products, arithmetic and copies ran while one was open for 2% of the time, Pallas kernels for 0%

profile of v1, /device:TPU:1, one launch (start us, length us, event | category | flops | bytes accessed | tf_op | source)
XLA Modules:
  0.0 58.4 jit_solution(7779684331260189151)
XLA Ops:
  0.0 0.0 copy-start.3
  0.0 0.0 copy-start.5
  0.0 0.0 copy-start.4
  0.0 0.0 copy-start.1
  0.0 2.7 %collective-permute-start.1 = (f32[1280,128]{1,0:T(8,128)}, f32[1280,128]{1,0:T(8,128)S(1)}, u32[]{:S(2)}, u32[]{:S(2)}) collective-permute-start(f32[1280,128]{1,0:T(8,128)} %bitcast.30), channel_id=1, source_target_pairs={{0,15},{1,2},{2,1},{3,4},{4,3},{5,6},{6,5},{7,8},{8,7},{9,10},{10,... | collective-permute-start | bytes 1966088 | tf_op jit(solution)/shard_map/ppermute | solution.py:134
  2.7 2.9 %collective-permute-start = (f32[1280,128]{1,0:T(8,128)}, f32[1280,128]{1,0:T(8,128)S(1)}, u32[]{:S(2)}, u32[]{:S(2)}) collective-permute-start(f32[1280,128]{1,0:T(8,128)} %bitcast.31), channel_id=1, source_target_pairs={{0,1},{1,0},{2,3},{3,2},{4,5},{5,4},{6,7},{7,6},{8,9},{9,8},{10,11... | collective-permute-start | bytes 1966088 | tf_op jit(solution)/shard_map/ppermute | solution.py:135
  5.6 0.7 %fusion = s32[2,4,128]{2,1,0:T(4,128)S(1)} fusion(s32[2,128,4]{1,2,0:T(4,128)} %param.10, s32[]{:T(128)S(6)} %xor.3, s32[]{:T(128)S(6)} %axis_index.12), kind=kLoop, calls=%fused_computation.5 | loop fusion | flops 25600 | bytes 8200 | tf_op jit(solution)/shard_map/add | solution.py:151
  6.3 11.9 %collective-permute-done.1.far = f32[1280,128]{1,0:T(8,128)S(1)} collective-permute-done((f32[1280,128]{1,0:T(8,128)}, f32[1280,128]{1,0:T(8,128)S(1)}, u32[]{:S(2)}, u32[]{:S(2)}) %collective-permute-start.1) | collective-permute-done | bytes 655392 | tf_op jit(solution)/shard_map/ppermute | solution.py:134
  18.2 0.0 collective-permute-done.near
  18.2 0.0 copy-start
  18.2 1.1 %copy-done = f32[128,10,128]{2,0,1:T(8,128)S(1)} copy-done((f32[128,10,128]{2,0,1:T(8,128)S(1)}, f32[128,10,128]{2,0,1:T(8,128)}, u32[]{:S(2)}) %copy-start) | copy-done | bytes 655384
  19.3 0.0 copy-start.2
  19.3 10.2 %step_one.1.own = f32[1280,128]{1,0:T(8,128)S(1)} custom-call(s32[4,128]{1,0:T(4,128)S(1)} %get-tuple-element.5.slots, f32[1280,128]{1,0:T(8,128)S(1)} %bitcast.32, f32[1280,128]{1,0:T(8,128)S(1)} %collective-permute-done.near, f32[1280,128]{1,0:T(8,128)S(1)} %collective-permute-done.1.far, bf16[2,128,4,128,128]{4,3,2,1,0:T(8,128)(2,1)} %transport.3), custom_call_target="tpu_custom_call" | custom-call | flops 335544320 | bytes 16777216 | tf_op jit(solution)/shard_map/step_one/pallas_call | solution.py:165
  29.5 1.8 %collective-permute-start.3 = (f32[1280,128]{1,0:T(8,128)S(1)}, f32[1280,128]{1,0:T(8,128)S(1)}, u32[]{:S(2)}, u32[]{:S(2)}) collective-permute-start(f32[1280,128]{1,0:T(8,128)S(1)} %step_one.1.own), channel_id=1, source_target_pairs={{0,15},{1,2},{2,1},{3,4},{4,3},{5,6},{6,5},{7,8},{8,7},{9,10},{10,... | collective-permute-start | bytes 1966088 | tf_op jit(solution)/shard_map/ppermute | solution.py:134
  31.3 0.0 collective-permute-start.2
  31.3 0.0 copy-done.3
  31.3 0.1 copy.13
  31.4 0.0 copy-done.5
  31.4 0.0 copy-done.4
  31.4 0.1 copy.11
  31.5 0.1 reshape.17.order
  31.6 0.0 copy-done.2
  31.7 12.9 %collective-permute-done.3.far = f32[1280,128]{1,0:T(8,128)S(1)} collective-permute-done((f32[1280,128]{1,0:T(8,128)S(1)}, f32[1280,128]{1,0:T(8,128)S(1)}, u32[]{:S(2)}, u32[]{:S(2)}) %collective-permute-start.3) | collective-permute-done | bytes 655392 | tf_op jit(solution)/shard_map/ppermute | solution.py:134
  44.6 0.0 collective-permute-done.2.near
  44.6 0.1 mul.23.sink
  44.7 0.1 mul.22.mix
  44.7 0.0 copy-done.1
  44.7 13.6 %step_two_columns.1 = f32[1280,128]{1,0:T(8,128)} custom-call(s32[4,128]{1,0:T(4,128)S(1)} %get-tuple-element.6.slots, s32[128]{0:T(128)S(1)} %reshape.17.order, f32[1280,128]{1,0:T(8,128)S(1)} %step_one.1.own, f32[1280,128]{1,0:T(8,128)S(1)} %collective-permute-done.2.near, f32[1280,128]{1,0:T(8,128)S(1)} %collective-permute-done.3.far, ...), custom_call_target="tpu_custom_call" | custom-call | flops 335544320 | bytes 16777216 | tf_op jit(solution)/shard_map/step_two_columns/pallas_call | solution.py:177
  (5 shorter events, 0.0 us)
Async XLA Ops:
  0.0 31.3 %copy-start.3 = (f32[10,10]{1,0:T(8,128)S(1)}, f32[10,10]{1,0:T(8,128)}, u32[]{:S(2)}) copy-start(f32[10,10]{1,0:T(8,128)} %param.14) | copy-start | bytes 1204
  0.0 31.4 %copy-start.5 = (f32[10]{0:T(128)S(1)}, f32[10]{0:T(128)}, u32[]{:S(2)}) copy-start(f32[10]{0:T(128)} %param.15) | copy-start | bytes 124
  0.0 31.4 %copy-start.4 = (s32[32,4]{0,1:T(4,128)S(1)}, s32[32,4]{0,1:T(4,128)}, u32[]{:S(2)}) copy-start(s32[32,4]{0,1:T(4,128)} %param.11) | copy-start | bytes 1540
  0.0 44.7 %copy-start.1 = (s32[512]{0:T(512)S(1)}, s32[512]{0:T(512)}, u32[]{:S(2)}) copy-start(s32[512]{0:T(512)} %param.12) | copy-start | bytes 6148
  0.0 18.2 %collective-permute-start.1 = (f32[1280,128]{1,0:T(8,128)}, f32[1280,128]{1,0:T(8,128)S(1)}, u32[]{:S(2)}, u32[]{:S(2)}) collective-permute-start(f32[1280,128]{1,0:T(8,128)} %bitcast.30), channel_id=1, source_target_pairs={{0,15},{1,2},{2,1},{3,4},{4,3},{5,6},{6,5},{7,8},{8,7},{9,10},{10,... | collective-permute-start | bytes 1966088 | tf_op jit(solution)/shard_map/ppermute | solution.py:134
  2.7 15.5 %collective-permute-start = (f32[1280,128]{1,0:T(8,128)}, f32[1280,128]{1,0:T(8,128)S(1)}, u32[]{:S(2)}, u32[]{:S(2)}) collective-permute-start(f32[1280,128]{1,0:T(8,128)} %bitcast.31), channel_id=1, source_target_pairs={{0,1},{1,0},{2,3},{3,2},{4,5},{5,4},{6,7},{7,6},{8,9},{9,8},{10,11... | collective-permute-start | bytes 1966088 | tf_op jit(solution)/shard_map/ppermute | solution.py:135
  18.2 1.1 %copy-start = (f32[128,10,128]{2,0,1:T(8,128)S(1)}, f32[128,10,128]{2,0,1:T(8,128)}, u32[]{:S(2)}) copy-start(f32[128,10,128]{2,0,1:T(8,128)} %param.8) | copy-start | bytes 1966084
  19.3 12.3 %copy-start.2 = (f32[32,512]{1,0:T(8,128)S(1)}, f32[32,512]{1,0:T(8,128)}, u32[]{:S(2)}) copy-start(f32[32,512]{1,0:T(8,128)} %param.13) | copy-start | bytes 196612
  29.5 15.1 %collective-permute-start.3 = (f32[1280,128]{1,0:T(8,128)S(1)}, f32[1280,128]{1,0:T(8,128)S(1)}, u32[]{:S(2)}, u32[]{:S(2)}) collective-permute-start(f32[1280,128]{1,0:T(8,128)S(1)} %step_one.1.own), channel_id=1, source_target_pairs={{0,15},{1,2},{2,1},{3,4},{4,3},{5,6},{6,5},{7,8},{8,7},{9,10},{10,... | collective-permute-start | bytes 1966088 | tf_op jit(solution)/shard_map/ppermute | solution.py:134
  31.3 13.3 %collective-permute-start.2 = (f32[1280,128]{1,0:T(8,128)S(1)}, f32[1280,128]{1,0:T(8,128)S(1)}, u32[]{:S(2)}, u32[]{:S(2)}) collective-permute-start(f32[1280,128]{1,0:T(8,128)S(1)} %step_one.1.own), channel_id=1, source_target_pairs={{0,1},{1,0},{2,3},{3,2},{4,5},{5,4},{6,7},{7,6},{8,9},{9,8},{10,11... | collective-permute-start | bytes 1966088 | tf_op jit(solution)/shard_map/ppermute | solution.py:135

commit v2 on v1

v2 whole, which is shorter than its diff:
```python
import functools

import jax
import jax.numpy as jnp
from jax import lax
from jax.experimental import pallas as pl
from jax.experimental.pallas import tpu as pltpu
from jax.sharding import PartitionSpec as P

GROUP = 32
CHUNK = 8
LIST = 8
LATE_GROUP = 32
UNROLL = True
DIRECT = 2
SPAN = 4096
NOTHING = 2048
ROWS = 16
VMEM_LIMIT = 12 * 1024 * 1024


def dot_nt(x, t):
    return lax.dot_general(x, t, (((1,), (1,)), ((), ())), preferred_element_type=jnp.float32)


def split_rows(field, row, tiles):
    x = field[pl.ds(row, ROWS, stride=tiles), :]
    high = x.astype(jnp.bfloat16)
    low = (x - high.astype(jnp.float32)).astype(jnp.bfloat16)
    return jnp.concatenate([high, low], axis=0)


def tile_product(slots, field, blocks, t, tiles, nb):
    xs = [split_rows(field, slots[b, t], tiles) for b in range(nb)]
    ts = [blocks[t, b] for b in range(nb)]
    acc = dot_nt(jnp.concatenate(xs, axis=1), jnp.concatenate(ts, axis=1))
    return acc[:ROWS] + acc[ROWS:]


def copy_rows(refs, field, sem):
    copies, row = [], 0
    for i, ref in enumerate(refs):
        copies.append(pltpu.make_async_copy(ref, field.at[pl.ds(row, ref.shape[0])], sem.at[i]))
        row += ref.shape[0]
    for copy in copies:
        copy.start()
    return copies


def block_copy(transport, which, blocks, sem, c):
    at = pl.ds(c * CHUNK, CHUNK)
    return pltpu.make_async_copy(transport.at[which, at], blocks.at[at], sem.at[c])


def prepare_kernel(tiles, ntr, regions, picks_in, order_in, rates_in, coupling_in, sinking, transport,
                   blocks, slots, later_slots, level_rates, mix, sink, picks, order, rates, coupling, sem, ssem):
    chunks = tiles // CHUNK
    small = [pltpu.make_async_copy(src, dst, ssem.at[i]) for i, (src, dst) in enumerate(
        ((picks_in, picks), (order_in, order), (rates_in, rates), (coupling_in, coupling)))]
    for copy in small:
        copy.start()
    for c in range(chunks):
        block_copy(transport, 0, blocks, sem, c).start()
    here = lax.axis_index("region")
    odd = lax.rem(here, 2)
    near = here + 1 - 2 * odd
    far = lax.rem(here + 2 * odd - 1 + regions, regions)
    rows = ntr * tiles
    for copy in small:
        copy.wait()
    nb = picks.shape[1]
    for step, table in enumerate((slots, later_slots)):
        p = picks[step]
        in_here = (p >= here * tiles) & (p < (here + 1) * tiles)
        in_near = (p >= near * tiles) & (p < (near + 1) * tiles)
        table[0:nb, :] = jnp.where(in_here, p - here * tiles,
                                   jnp.where(in_near, p - near * tiles + rows, p - far * tiles + 2 * rows))
    later_slots[nb:, :] = jnp.zeros((later_slots.shape[0] - nb, later_slots.shape[1]), jnp.int32)
    later_slots[nb:nb + order.shape[0], 0:order.shape[1]] = order[...] - here * tiles
    for q in range(level_rates.shape[1]):
        level_rates[:, q, :] = rates[:, q * 128:(q + 1) * 128]
    mix[...] = jnp.zeros_like(mix)
    sink[...] = jnp.zeros_like(sink)
    for s in range(ntr):
        mix[s, 0:ntr, :] = jnp.broadcast_to(coupling[:, s:s + 1], (ntr, 128))
        sink[s:s + 1, :] = jnp.full((1, 128), sinking[s], jnp.float32)
    for c in range(chunks):
        block_copy(transport, 0, blocks, sem, c).wait()


def first_kernel(tiles, nb, ntr, slots, own, near, far, blocks, transport, out, later_blocks, field, fsem, bsem):
    copies = copy_rows((own, near, far), field, fsem)
    chunks = tiles // CHUNK
    for c in range(chunks):
        block_copy(transport, 1, later_blocks, bsem, c).start()
    for copy in copies:
        copy.wait()

    def step(c, _):
        for u in range(GROUP):
            t = c * GROUP + u
            v = tile_product(slots, field, blocks, t, tiles, nb)
            out[pl.ds(t, ntr, stride=tiles), :] = v[:ntr]
        return 0

    lax.fori_loop(0, tiles // GROUP, step, 0)
    for c in range(chunks):
        block_copy(transport, 1, later_blocks, bsem, c).wait()


def early_kernel(tiles, nb, ntr, levels, slots, own, near, near_end, blocks, partial, table, field, fsem):
    copies = copy_rows((own, near, near_end), field, fsem)
    rows = ntr * tiles
    field[2 * rows:, :] = jnp.zeros((field.shape[0] - 2 * rows, 128), jnp.float32)
    for copy in copies:
        copy.wait()
    order_at, count_at, list_at = table_places(tiles, nb)
    col_blocks = tiles // levels

    def step(c, n):
        for u in range(GROUP):
            t = c * GROUP + u
            partial[t] = tile_product(slots, field, blocks, t, tiles, nb)
            used = jnp.int32(0)
            for b in range(nb):
                p = slots[b, t] - 2 * rows
                table[used * tiles + t] = b * SPAN + p
                used = used + (p >= 0).astype(jnp.int32)
            for b in range(DIRECT):
                table[(used + b) * tiles + t] = NOTHING
            for b in range(DIRECT, nb):
                table[list_at + n] = t * (nb * SPAN) + table[b * tiles + t]
                n = n + (used > b).astype(jnp.int32)
        return n

    n = lax.fori_loop(0, tiles // GROUP, step, jnp.int32(0))
    table[count_at] = n
    for i in range(LIST):
        table[list_at + n + i] = NOTHING

    def move(k, _):
        for q in range(col_blocks):
            table[order_at + k * col_blocks + q] = slots[nb + q, k]
        return 0

    lax.fori_loop(0, levels, move, 0)


def table_places(tiles, nb):
    order_at = (nb + DIRECT) * tiles
    count_at = order_at + tiles
    return order_at, count_at, count_at + tiles


def late_kernel(tiles, nb, ntr, levels, table, far, partial, blocks, rates, depths, mix, sink,
                out, field, total, value, fsem, tsem):
    order_at, count_at, list_at = table_places(tiles, nb)
    whole = pltpu.make_async_copy(partial, total, tsem)
    whole.start()
    copies = copy_rows((far,), field, fsem)
    field[NOTHING:, :] = jnp.zeros((field.shape[0] - NOTHING, 128), jnp.float32)
    for copy in copies:
        copy.wait()
    whole.wait()

    def place(e):
        return lax.div(e, SPAN), lax.rem(e, SPAN)

    def rest(i, _):
        found = []
        for u in range(LIST):
            block, row = place(table[list_at + i * LIST + u])
            t = block // nb
            r = dot_nt(split_rows(field, row, tiles), blocks[t, lax.rem(block, nb)])
            found.append((t, r[:ROWS] + r[ROWS:]))
        for t, r in found:
            total[t] += r
        return 0

    lax.fori_loop(0, lax.div(table[count_at] + LIST - 1, LIST), rest, 0)

    col_blocks = tiles // levels
    per = LATE_GROUP // col_blocks
    steps = tiles // LATE_GROUP

    def products(c):
        for u in range(LATE_GROUP):
            t = table[order_at + c * LATE_GROUP + u]
            xs, ts = [], []
            for m in range(DIRECT):
                b, row = place(table[m * tiles + t])
                xs.append(split_rows(field, row, tiles))
                ts.append(blocks[t, b])
            r = dot_nt(jnp.concatenate(xs, axis=1), jnp.concatenate(ts, axis=1))
            value[c % 2 if isinstance(c, int) else lax.rem(c, 2), u] = r[:ROWS] + r[ROWS:] + total[t]

    def chain(c, carry):
        carry = list(carry)
        for l in range(per):
            k = c * per + l
            for q in range(col_blocks):
                u = l * col_blocks + q
                t = table[order_at + c * LATE_GROUP + u]
                v = value[c % 2 if isinstance(c, int) else lax.rem(c, 2), u]
                mixed = mix[0] * v[0:1]
                for s in range(1, ntr):
                    mixed = mixed + mix[s] * v[s:s + 1]
                wet = k < depths[:, q * 128:(q + 1) * 128]
                y = jnp.where(wet, v + rates[k, q:q + 1] * mixed + carry[q], jnp.float32(0.0))
                carry[q] = sink[...] * y
                out[pl.ds(t, ntr, stride=tiles), :] = y[:ntr]
        return tuple(carry)

    carry = tuple(jnp.zeros((ROWS, 128), jnp.float32) for _ in range(col_blocks))
    products(0)

    def step(c, carry):
        products(c)
        return chain(c - 1, carry)

    if UNROLL:
        for c in range(1, steps):
            carry = step(c, carry)
    else:
        carry = lax.fori_loop(1, steps, step, carry)
    chain(steps - 1, carry)


def exchange(rows):
    n = lax.axis_size("region")
    near = [(i, i ^ 1) for i in range(n)]
    far = [(i, (i + 1) % n if i % 2 else (i - 1) % n) for i in range(n)]
    b = lax.ppermute(rows, "region", far)
    a = lax.ppermute(rows, "region", near)
    return a, b


def exchange_split(rows):
    n = lax.axis_size("region")
    near = [(i, i ^ 1) for i in range(n)]
    far = [(i, (i + 1) % n if i % 2 else (i - 1) % n) for i in range(n)]
    b = lax.ppermute(rows, "region", far)
    half = rows.shape[0] // 2
    a = [lax.ppermute(rows[i * half:(i + 1) * half], "region", near) for i in range(2)]
    return a, b


def shards(tangent, transport, block_column, cell_order, depths, rates, coupling, sinking):
    tiles, ntr, cells = tangent.shape
    nb = block_column.shape[2]
    levels, col_blocks = cell_order.shape
    rows = ntr * tiles
    chunks = tiles // CHUNK
    planar = jnp.transpose(tangent, (1, 0, 2)).reshape(rows, cells)
    near, far = exchange(planar)

    smem = pl.BlockSpec(memory_space=pltpu.SMEM)
    vmem = pl.BlockSpec(memory_space=pltpu.VMEM)
    anyw = pl.BlockSpec(memory_space=pl.ANY)
    params = pltpu.CompilerParams(vmem_limit_bytes=VMEM_LIMIT)
    cost = pl.CostEstimate(
        flops=4 * tiles * nb * cells * cells * ntr, bytes_accessed=transport.size, transcendentals=0
    )
    f32, i32 = jnp.float32, jnp.int32
    array = jax.ShapeDtypeStruct
    blocks_shape = pltpu.VMEM(transport.shape[1:], transport.dtype)
    pad = (ROWS - ntr) * tiles
    sems = pltpu.SemaphoreType.DMA

    hbm = pl.BlockSpec(memory_space=pltpu.HBM)
    first_blocks, first_slots, second_slots, level_rates, mix, sink = pl.pallas_call(
        functools.partial(prepare_kernel, tiles, ntr, lax.axis_size("region")),
        out_shape=(
            blocks_shape,
            array((nb, tiles), i32),
            array((nb + max(nb, col_blocks), tiles), i32),
            array((levels, col_blocks, cells), f32),
            array((ntr, ROWS, cells), f32),
            array((ROWS, cells), f32),
        ),
        in_specs=[hbm, hbm, hbm, hbm, smem, anyw],
        out_specs=[vmem] * 6,
        scratch_shapes=[
            pltpu.VMEM((2, nb, tiles), i32),
            pltpu.VMEM((col_blocks, levels), i32),
            pltpu.VMEM(rates.shape, f32),
            pltpu.VMEM(coupling.shape, f32),
            sems((chunks,)),
            sems((4,)),
        ],
        compiler_params=params,
        cost_estimate=cost,
        name="prepare",
    )(jnp.transpose(block_column, (0, 2, 1)), cell_order.T, rates, coupling, sinking, transport)

    middle, second_blocks = pl.pallas_call(
        functools.partial(first_kernel, tiles, nb, ntr),
        out_shape=(array((rows, cells), f32), blocks_shape),
        in_specs=[smem, anyw, anyw, anyw, vmem, anyw],
        out_specs=[vmem, vmem],
        scratch_shapes=[pltpu.VMEM((3 * rows + pad, cells), f32), sems((3,)), sems((chunks,))],
        compiler_params=params,
        cost_estimate=cost,
        name="step_one",
    )(first_slots, pltpu.with_memory_space_constraint(planar, pltpu.VMEM), near, far, first_blocks, transport)

    near, far = exchange_split(middle)
    table_size = table_places(tiles, nb)[2] + (nb - DIRECT) * tiles + LIST
    partial, table = pl.pallas_call(
        functools.partial(early_kernel, tiles, nb, ntr, levels),
        out_shape=(array((tiles, ROWS, cells), f32), array((table_size,), i32)),
        in_specs=[smem, anyw, anyw, anyw, vmem],
        out_specs=[vmem, smem],
        scratch_shapes=[pltpu.VMEM((3 * rows + pad, cells), f32), sems((3,))],
        compiler_params=params,
        cost_estimate=pl.CostEstimate(flops=0, bytes_accessed=0, transcendentals=0),
        name="step_two_early",
    )(second_slots, middle, *near, second_blocks)

    result = pl.pallas_call(
        functools.partial(late_kernel, tiles, nb, ntr, levels),
        out_shape=array((rows, cells), f32),
        in_specs=[smem, anyw] + [vmem] * 6,
        out_specs=vmem,
        scratch_shapes=[
            pltpu.VMEM((2 * NOTHING, cells), f32),
            pltpu.VMEM((tiles, ROWS, cells), f32),
            pltpu.VMEM((2, LATE_GROUP, ROWS, cells), f32),
            sems((1,)),
            sems,
        ],
        compiler_params=params,
        cost_estimate=cost,
        name="step_two_late",
    )(table, far, partial, second_blocks, level_rates, depths.reshape(1, -1), mix, sink)
    return jnp.transpose(result.reshape(ntr, tiles, cells), (1, 0, 2))


def solution(mesh):
    in_specs = (
        P(("groups", "region"), None, None),
        P(None, "region", None, None, None),
        P(None, "region", None),
        P(None, "region"),
        P("region"),
        P(None, "region"),
        P(),
        P(),
    )
    out_specs = P(("groups", "region"), None, None)
    return jax.shard_map(shards, mesh=mesh, in_specs=in_specs, out_specs=out_specs, check_vma=False)
```

time: 58.5 us -> 49.4 us (0.84)
  waiting for transfers between devices: 24.8 us -> 8.72 us
  Pallas kernels: 23.8 us -> 29.1 us
  local copies, waits for them, and re-layouts: 1.57 us -> 3.61 us
  other arithmetic: 0.71 us -> 0 us
    ppermute x2 -> x1, waiting for transfers between devices: 24.8 us -> 2.45 us  [exchange(): b = lax.ppermute(rows, 'region', far)]
    pallas_call x1 -> x3, Pallas kernels: 13.6 us -> 21.4 us  [the longest x1 7.99 us: shards(): pl.pallas_call(functools.partial(early_kernel, tiles, nb, ntr, levels), o...]
    ppermute x0 -> x3, waiting for transfers between devices: none -> 6.26 us  [the longest x1 4.68 us: exchange_split(): b = lax.ppermute(rows, 'region', far)]
    pallas_call x1, Pallas kernels: 10.2 us -> 7.63 us  [shards(): pl.pallas_call(functools.partial(first_kernel, tiles, nb, ntr), out_shape...]
    unnamed x13 -> x14, local copies, waits for them, and re-layouts: 1.2 us -> 3.57 us
    ppermute x0 -> x3, starting transfers between devices: none -> 2.36 us  [the longest x1 1.79 us: exchange_split(): b = lax.ppermute(rows, 'region', far)]
    ppermute x2 -> x1, starting transfers between devices: 4.51 us -> 2.63 us  [exchange(): b = lax.ppermute(rows, 'region', far)]
    add x1 -> x0, other arithmetic: 0.7 us -> none  [shards(): slots = place * rows + picks % tiles]
  transfers between devices with their start and end apart: 4 -> 5, of which waited for: 2 -> 4; matrix products, arithmetic and copies ran while one was open for 2% -> 0% of each run, Pallas kernels for 0% -> 30%
where the time goes in v2:
time: 49.4 us; the launch traced here: 49.3 us
  Pallas kernels  29.1 us (59%)
  waiting for transfers between devices  8.72 us (18%)
  starting transfers between devices  7.86 us (16%)
  local copies, waits for them, and re-layouts  3.61 us (7%)
    pallas_call x1, Pallas kernels, shards(): pl.pallas_call(functools.partial(early_kernel, tiles, nb, ntr, levels), o...  7.99 us
    pallas_call x1, Pallas kernels, shards(): pl.pallas_call(functools.partial(first_kernel, tiles, nb, ntr), out_shape...  7.63 us
    pallas_call x1, Pallas kernels, shards(): pl.pallas_call(functools.partial(late_kernel, tiles, nb, ntr, levels), ou...  6.86 us
    pallas_call x1, Pallas kernels, shards(): pl.pallas_call(functools.partial(prepare_kernel, tiles, ntr, lax.axis_siz...  6.6 us
    ppermute x1, waiting for transfers between devices, exchange_split(): b = lax.ppermute(rows, 'region', far)  4.68 us
    unnamed x14, local copies, waits for them, and re-layouts  3.57 us
    ppermute x1, starting transfers between devices, exchange(): a = lax.ppermute(rows, 'region', near)  2.87 us
    ppermute x1, starting transfers between devices, exchange(): b = lax.ppermute(rows, 'region', far)  2.63 us
  transfers between devices with their start and end apart: 5, of which 4 were waited for; matrix products, arithmetic and copies ran while one was open for 0% of the time, Pallas kernels for 30%

profile of v2, /device:TPU:1, one launch (start us, length us, event | category | flops | bytes accessed | tf_op | source)
XLA Modules:
  0.0 49.3 jit_solution(10316996046153128961)
XLA Ops:
  0.0 2.6 %collective-permute-start.1 = (f32[1280,128]{1,0:T(8,128)}, f32[1280,128]{1,0:T(8,128)S(1)}, u32[]{:S(2)}, u32[]{:S(2)}) collective-permute-start(f32[1280,128]{1,0:T(8,128)} %bitcast.9), channel_id=1, source_target_pairs={{0,15},{1,2},{2,1},{3,4},{4,3},{5,6},{6,5},{7,8},{8,7},{9,10},{10,... | collective-permute-start | bytes 1966088 | tf_op jit(solution)/shard_map/ppermute | solution.py:233
  2.6 2.9 %collective-permute-start = (f32[1280,128]{1,0:T(8,128)}, f32[1280,128]{1,0:T(8,128)S(1)}, u32[]{:S(2)}, u32[]{:S(2)}) collective-permute-start(f32[1280,128]{1,0:T(8,128)} %bitcast.10), channel_id=1, source_target_pairs={{0,1},{1,0},{2,3},{3,2},{4,5},{5,4},{6,7},{7,6},{8,9},{9,8},{10,11... | collective-permute-start | bytes 1966088 | tf_op jit(solution)/shard_map/ppermute | solution.py:234
  5.5 0.0 copy-start.1
  5.5 0.8 %copy-done.1 = f32[32,512]{1,0:T(8,128)S(1)} copy-done((f32[32,512]{1,0:T(8,128)S(1)}, f32[32,512]{1,0:T(8,128)}, u32[]{:S(2)}) %copy-start.1) | copy-done | bytes 65560
  6.3 0.0 copy-start.2
  6.3 0.7 %copy-done.2 = f32[10,10]{1,0:T(8,128)S(1)} copy-done((f32[10,10]{1,0:T(8,128)S(1)}, f32[10,10]{1,0:T(8,128)}, u32[]{:S(2)}) %copy-start.2) | copy-done | bytes 424
  7.0 0.0 copy-start.3
  7.0 0.7 %copy-done.3 = s32[2,128,4]{1,2,0:T(4,128)S(1)} copy-done((s32[2,128,4]{1,2,0:T(4,128)S(1)}, s32[2,128,4]{1,2,0:T(4,128)}, u32[]{:S(2)}) %copy-start.3) | copy-done | bytes 4120
  7.7 0.0 copy-start.4
  7.7 0.7 %copy-done.4 = s32[32,4]{0,1:T(4,128)S(1)} copy-done((s32[32,4]{0,1:T(4,128)S(1)}, s32[32,4]{0,1:T(4,128)}, u32[]{:S(2)}) %copy-start.4) | copy-done | bytes 536
  8.4 0.0 copy-start.6
  8.4 0.7 %copy-done.6 = f32[10]{0:T(128)S(1)} copy-done((f32[10]{0:T(128)S(1)}, f32[10]{0:T(128)}, u32[]{:S(2)}) %copy-start.6) | copy-done | bytes 64
  9.1 0.0 copy-start
  9.1 6.6 %prepare.1 = (bf16[128,4,128,128]{3,2,1,0:T(8,128)(2,1)S(1)}, s32[4,128]{1,0:T(4,128)S(1)}, s32[8,128]{1,0:T(8,128)S(1)}, f32[32,4,128]{2,1,0:T(4,128)S(1)}, f32...) custom-call(s32[2,4,128]{2,1,0:T(4,128)S(1)} %bitcast.12, s32[4,32]{1,0:T(4,128)S(1)} %bitcast.13, ...), custom_call_target="tpu_custom_call" | custom-call | flops 335544320 | bytes 16777216 | tf_op jit(solution)/shard_map/prepare/pallas_call | solution.py:271
  15.7 2.5 %collective-permute-done.1.far = f32[1280,128]{1,0:T(8,128)S(1)} collective-permute-done((f32[1280,128]{1,0:T(8,128)}, f32[1280,128]{1,0:T(8,128)S(1)}, u32[]{:S(2)}, u32[]{:S(2)}) %collective-permute-start.1) | collective-permute-done | bytes 655392 | tf_op jit(solution)/shard_map/ppermute | solution.py:233
  18.1 0.0 collective-permute-done.near
  18.1 0.0 copy-done
  18.1 7.6 %step_one.1 = (f32[1280,128]{1,0:T(8,128)S(1)}, bf16[128,4,128,128]{3,2,1,0:T(8,128)(2,1)S(1)}) custom-call(s32[4,128]{1,0:T(4,128)S(1)} %get-tuple-element.16.slots, f32[1280,128]{1,0:T(8,128)S(1)} %bitcast.11, f32[1280,128]{1,0:T(8,128)S(1)} %collective-permute-done.near, f32[1280,128]{1,0:T(8,128)S(1)} %collective-permute-done.1.far, ...), custom_call_target="tpu_custom_call" | custom-call | flops 335544320 | bytes 16777216 | tf_op jit(solution)/shard_map/step_one/pallas_call | solution.py:296
  25.8 0.0 copy-start.5
  25.8 1.8 %collective-permute-start.4 = (f32[1280,128]{1,0:T(8,128)S(1)}, f32[1280,128]{1,0:T(8,128)S(1)}, u32[]{:S(2)}, u32[]{:S(2)}) collective-permute-start(f32[1280,128]{1,0:T(8,128)S(1)} %get-tuple-element.18.own), channel_id=1, source_target_pairs={{0,15},{1,2},{2,1},{3,4},{4,3},{5,6},{6,5},{7,8},{8,7},{9,10},{10,... | collective-permute-start | bytes 1966088 | tf_op jit(solution)/shard_map/ppermute | solution.py:242
  27.6 0.1 collective-permute-start.3
  27.7 0.5 %collective-permute-start.2 = (f32[640,128]{1,0:T(8,128)S(1)}, f32[640,128]{1,0:T(8,128)S(1)}, u32[]{:S(2)}, u32[]{:S(2)}) collective-permute-start(f32[640,128]{1,0:T(8,128)S(1)} %get-tuple-element.26), channel_id=1, source_target_pairs={{0,1},{1,0},{2,3},{3,2},{4,5},{5,4},{6,7},{7,6},{8,9},{9,8},{10,11... | collective-permute-start | bytes 983048 | tf_op jit(solution)/shard_map/ppermute | solution.py:244
  28.2 1.1 %collective-permute-done.3.near_end = f32[640,128]{1,0:T(8,128)S(1)} collective-permute-done((f32[640,128]{1,0:T(8,128)S(1)}, f32[640,128]{1,0:T(8,128)S(1)}, u32[]{:S(2)}, u32[]{:S(2)}) %collective-permute-start.3) | collective-permute-done | bytes 327712 | tf_op jit(solution)/shard_map/ppermute | solution.py:244
  29.3 0.5 collective-permute-done.2.near
  29.8 8.0 %step_two_early.1 = (f32[128,16,128]{2,1,0:T(8,128)S(1)}, s32[1288]{0:T(1024)S(1)}) custom-call(s32[8,128]{1,0:T(8,128)S(1)} %get-tuple-element.15.slots, f32[1280,128]{1,0:T(8,128)S(1)} %get-tuple-element.18.own, f32[640,128]{1,0:T(8,128)S(1)} %collective-permute-done.2.near, f32[640,128]{1,0:T(8,128)S(1)} %collective-permute-done.3.near_end, ...), custom_call_target="tpu_custom_call" | custom-call | tf_op jit(solution)/shard_map/step_two_early/pallas_call | solution.py:309
  37.8 4.7 %collective-permute-done.4.far = f32[1280,128]{1,0:T(8,128)S(1)} collective-permute-done((f32[1280,128]{1,0:T(8,128)S(1)}, f32[1280,128]{1,0:T(8,128)S(1)}, u32[]{:S(2)}, u32[]{:S(2)}) %collective-permute-start.4) | collective-permute-done | bytes 655392 | tf_op jit(solution)/shard_map/ppermute | solution.py:242
  42.5 0.0 copy-done.5
  42.5 6.9 %step_two_late.1 = f32[1280,128]{1,0:T(8,128)} custom-call(s32[1288]{0:T(1024)S(1)} %get-tuple-element.20.table, f32[1280,128]{1,0:T(8,128)S(1)} %collective-permute-done.4.far, f32[128,16,128]{2,1,0:T(8,128)S(1)} %get-tuple-element.21.partial, bf16[128,4,128,128]{3,2,1,0:T(8,128)(2,1)S(1)} %get-tuple-element.19.blocks, ...), custom_call_target="tpu_custom_call" | custom-call | flops 335544320 | bytes 16777216 | tf_op jit(solution)/shard_map/step_two_late/pallas_call | solution.py:320
  (1 shorter events, 0.0 us)
Async XLA Ops:
  0.0 18.1 %collective-permute-start.1 = (f32[1280,128]{1,0:T(8,128)}, f32[1280,128]{1,0:T(8,128)S(1)}, u32[]{:S(2)}, u32[]{:S(2)}) collective-permute-start(f32[1280,128]{1,0:T(8,128)} %bitcast.9), channel_id=1, source_target_pairs={{0,15},{1,2},{2,1},{3,4},{4,3},{5,6},{6,5},{7,8},{8,7},{9,10},{10,... | collective-permute-start | bytes 1966088 | tf_op jit(solution)/shard_map/ppermute | solution.py:233
  2.6 15.5 %collective-permute-start = (f32[1280,128]{1,0:T(8,128)}, f32[1280,128]{1,0:T(8,128)S(1)}, u32[]{:S(2)}, u32[]{:S(2)}) collective-permute-start(f32[1280,128]{1,0:T(8,128)} %bitcast.10), channel_id=1, source_target_pairs={{0,1},{1,0},{2,3},{3,2},{4,5},{5,4},{6,7},{7,6},{8,9},{9,8},{10,11... | collective-permute-start | bytes 1966088 | tf_op jit(solution)/shard_map/ppermute | solution.py:234
  5.5 0.8 %copy-start.1 = (f32[32,512]{1,0:T(8,128)S(1)}, f32[32,512]{1,0:T(8,128)}, u32[]{:S(2)}) copy-start(f32[32,512]{1,0:T(8,128)} %rates_in.1) | copy-start | bytes 196612
  6.3 0.7 %copy-start.2 = (f32[10,10]{1,0:T(8,128)S(1)}, f32[10,10]{1,0:T(8,128)}, u32[]{:S(2)}) copy-start(f32[10,10]{1,0:T(8,128)} %coupling_in.1) | copy-start | bytes 1204
  7.0 0.7 %copy-start.3 = (s32[2,128,4]{1,2,0:T(4,128)S(1)}, s32[2,128,4]{1,2,0:T(4,128)}, u32[]{:S(2)}) copy-start(s32[2,128,4]{1,2,0:T(4,128)} %param.10) | copy-start | bytes 12292
  7.7 0.7 %copy-start.4 = (s32[32,4]{0,1:T(4,128)S(1)}, s32[32,4]{0,1:T(4,128)}, u32[]{:S(2)}) copy-start(s32[32,4]{0,1:T(4,128)} %param.11) | copy-start | bytes 1540
  8.4 0.7 %copy-start.6 = (f32[10]{0:T(128)S(1)}, f32[10]{0:T(128)}, u32[]{:S(2)}) copy-start(f32[10]{0:T(128)} %sinking.1) | copy-start | bytes 124
  9.1 9.1 %copy-start = (f32[128,10,128]{2,0,1:T(8,128)S(1)}, f32[128,10,128]{2,0,1:T(8,128)}, u32[]{:S(2)}) copy-start(f32[128,10,128]{2,0,1:T(8,128)} %param.8) | copy-start | bytes 1966084
  25.8 16.7 %copy-start.5 = (s32[512]{0:T(512)S(1)}, s32[512]{0:T(512)}, u32[]{:S(2)}) copy-start(s32[512]{0:T(512)} %param.12) | copy-start | bytes 6148
  25.8 16.7 %collective-permute-start.4 = (f32[1280,128]{1,0:T(8,128)S(1)}, f32[1280,128]{1,0:T(8,128)S(1)}, u32[]{:S(2)}, u32[]{:S(2)}) collective-permute-start(f32[1280,128]{1,0:T(8,128)S(1)} %get-tuple-element.18.own), channel_id=1, source_target_pairs={{0,15},{1,2},{2,1},{3,4},{4,3},{5,6},{6,5},{7,8},{8,7},{9,10},{10,... | collective-permute-start | bytes 1966088 | tf_op jit(solution)/shard_map/ppermute | solution.py:242
  27.6 1.7 %collective-permute-start.3 = (f32[640,128]{1,0:T(8,128)S(1)}, f32[640,128]{1,0:T(8,128)S(1)}, u32[]{:S(2)}, u32[]{:S(2)}) collective-permute-start(f32[640,128]{1,0:T(8,128)S(1)} %get-tuple-element.25), channel_id=1, source_target_pairs={{0,1},{1,0},{2,3},{3,2},{4,5},{5,4},{6,7},{7,6},{8,9},{9,8},{10,11... | collective-permute-start | bytes 983048 | tf_op jit(solution)/shard_map/ppermute | solution.py:244
  27.7 2.1 %collective-permute-start.2 = (f32[640,128]{1,0:T(8,128)S(1)}, f32[640,128]{1,0:T(8,128)S(1)}, u32[]{:S(2)}, u32[]{:S(2)}) collective-permute-start(f32[640,128]{1,0:T(8,128)S(1)} %get-tuple-element.26), channel_id=1, source_target_pairs={{0,1},{1,0},{2,3},{3,2},{4,5},{5,4},{6,7},{7,6},{8,9},{9,8},{10,11... | collective-permute-start | bytes 983048 | tf_op jit(solution)/shard_map/ppermute | solution.py:244

commit v3 on v2

v3 whole, which is shorter than its diff:
```python
import functools

import jax
import jax.numpy as jnp
from jax import lax
from jax.experimental import pallas as pl
from jax.experimental.pallas import tpu as pltpu
from jax.sharding import PartitionSpec as P

GROUP = 16
CHUNK = 8
LIST = 8
LATE_GROUP = 16
UNROLL = True
DIRECT = 2
SPAN = 4096
NOTHING = 2048
ROWS = 16
VMEM_LIMIT = 12 * 1024 * 1024


def dot_nt(x, t):
    return lax.dot_general(x, t, (((1,), (1,)), ((), ())), preferred_element_type=jnp.float32)


def split_rows(field, row, tiles):
    x = field[pl.ds(row, ROWS, stride=tiles), :]
    high = x.astype(jnp.bfloat16)
    low = (x - high.astype(jnp.float32)).astype(jnp.bfloat16)
    return jnp.concatenate([high, low], axis=0)


def copy_rows(refs, field, sem):
    copies, row = [], 0
    for i, ref in enumerate(refs):
        copies.append(pltpu.make_async_copy(ref, field.at[pl.ds(row, ref.shape[0])], sem.at[i]))
        row += ref.shape[0]
    for copy in copies:
        copy.start()
    return copies


def block_copy(transport, which, blocks, sem, c):
    at = pl.ds(c * CHUNK, CHUNK)
    return pltpu.make_async_copy(transport.at[which, at], blocks.at[at], sem.at[c])


def split_index(index, size):
    if size & (size - 1) == 0:
        high = lax.shift_right_logical(index, jnp.int32(size.bit_length() - 1))
    else:
        high = lax.div(index, jnp.int32(size))
    return high, index - high * size


def table_rows(nb, col_blocks):
    order_row = 2 * nb
    list_row = order_row + col_blocks
    return order_row, list_row, list_row + nb


def index_table(tiles, nb, ntr, regions, picks, staged):
    here = lax.axis_index("region")
    odd = lax.rem(here, 2)
    near = here + 1 - 2 * odd
    far = lax.rem(here + 2 * odd - 1 + regions, regions)
    rows = ntr * tiles
    staged[...] = jnp.zeros_like(staged)
    chosen = [jnp.full((1, tiles), NOTHING, jnp.int32) for _ in range(nb)]
    used = jnp.zeros((1, tiles), jnp.int32)
    for b in range(nb):
        p = picks[b:b + 1, :]
        in_here = (p >= here * tiles) & (p < (here + 1) * tiles)
        in_near = (p >= near * tiles) & (p < (near + 1) * tiles)
        distant = jnp.where(in_here | in_near, 0, 1)
        away = p - far * tiles
        staged[b:b + 1, :] = jnp.where(in_here, p - here * tiles, jnp.where(in_near, p - near * tiles + rows, 2 * rows))
        for m in range(b + 1):
            chosen[m] = jnp.where((distant == 1) & (used == m), away + b * SPAN, chosen[m])
        used = used + distant
    for m in range(nb):
        staged[nb + m:nb + m + 1, :] = chosen[m]
    return here


def early_products(tiles, nb, col_blocks, table, field, blocks, partial, ready):
    order_row, list_row, count_row = table_rows(nb, col_blocks)

    def put(n, e):
        row, lane = split_index(n, tiles)
        table[list_row + row, lane] = e

    def step(c, n):
        ready(c)
        for u in range(GROUP):
            t = c * GROUP + u
            xs = [split_rows(field, table[b, t], tiles) for b in range(nb)]
            for m in range(DIRECT, nb):
                e = table[nb + m, t]
                put(n, t * (nb * SPAN) + e)
                n = n + jnp.where(e == NOTHING, 0, 1).astype(jnp.int32)
            r = dot_nt(jnp.concatenate(xs, axis=1), jnp.concatenate([blocks[t, b] for b in range(nb)], axis=1))
            partial[t] = r[:ROWS] + r[ROWS:]
        return n

    n = lax.fori_loop(0, tiles // GROUP, step, jnp.int32(0))
    table[count_row, 0] = n
    for i in range(LIST):
        put(n + i, NOTHING)


def early_first_kernel(tiles, nb, ntr, col_blocks, regions, picks_in, own, near, transport, blocks, partial, table,
                       picks, staged, field, psem, fsem, bsem):
    index = pltpu.make_async_copy(picks_in.at[0], picks, psem)
    index.start()
    copies = copy_rows((own, near), field, fsem)
    for c in range(tiles // CHUNK):
        block_copy(transport, 0, blocks, bsem, c).start()
    rows = ntr * tiles
    field[2 * rows:, :] = jnp.zeros((field.shape[0] - 2 * rows, 128), jnp.float32)
    index.wait()
    index_table(tiles, nb, ntr, regions, picks, staged)
    index = pltpu.make_async_copy(staged, table, psem)
    index.start()
    for copy in copies:
        copy.wait()
    index.wait()

    def ready(c):
        for i in range(GROUP // CHUNK):
            block_copy(transport, 0, blocks, bsem, c * (GROUP // CHUNK) + i).wait()

    early_products(tiles, nb, col_blocks, table, field, blocks, partial, ready)


def early_second_kernel(tiles, nb, ntr, col_blocks, regions, picks_in, order_in, rates_in, coupling_in, sinking,
                        own, near, near_end, transport, blocks, partial, table, level_rates, mix, sink,
                        picks, staged, field, order, rates, coupling, psem, fsem, ssem, bsem):
    index = pltpu.make_async_copy(picks_in.at[1], picks, psem)
    index.start()
    small = [pltpu.make_async_copy(src, dst, ssem.at[i]) for i, (src, dst) in enumerate(
        ((order_in, order), (rates_in, rates), (coupling_in, coupling)))]
    for copy in small:
        copy.start()
    copies = copy_rows((own, near, near_end), field, fsem)
    for c in range(tiles // CHUNK):
        block_copy(transport, 1, blocks, bsem, c).start()
    rows = ntr * tiles
    field[2 * rows:, :] = jnp.zeros((field.shape[0] - 2 * rows, 128), jnp.float32)
    index.wait()
    for copy in small:
        copy.wait()
    here = index_table(tiles, nb, ntr, regions, picks, staged)
    order_row = table_rows(nb, col_blocks)[0]
    staged[order_row:order_row + col_blocks, 0:order.shape[1]] = order[...] - here * tiles
    index = pltpu.make_async_copy(staged, table, psem)
    index.start()
    for q in range(col_blocks):
        level_rates[:, q, :] = rates[:, q * 128:(q + 1) * 128]
    mix[...] = jnp.zeros_like(mix)
    sink[...] = jnp.zeros_like(sink)
    for s in range(ntr):
        mix[s, 0:ntr, :] = jnp.broadcast_to(coupling[:, s:s + 1], (ntr, 128))
        sink[s:s + 1, :] = jnp.full((1, 128), sinking[s], jnp.float32)
    for copy in copies:
        copy.wait()
    index.wait()

    def ready(c):
        for i in range(GROUP // CHUNK):
            block_copy(transport, 1, blocks, bsem, c * (GROUP // CHUNK) + i).wait()

    early_products(tiles, nb, col_blocks, table, field, blocks, partial, ready)


def place(e):
    return split_index(e, SPAN)


def far_product(tiles, nb, table, field, blocks, t):
    xs, ts = [], []
    for m in range(DIRECT):
        b, row = place(table[nb + m, t])
        xs.append(split_rows(field, row, tiles))
        ts.append(blocks[t, b])
    r = dot_nt(jnp.concatenate(xs, axis=1), jnp.concatenate(ts, axis=1))
    return r[:ROWS] + r[ROWS:]


def load_far(tiles, nb, col_blocks, table, far, blocks, field, total, fsem):
    order_row, list_row, count_row = table_rows(nb, col_blocks)
    copies = copy_rows((far,), field, fsem)
    total[...] = jnp.zeros_like(total)
    field[NOTHING:, :] = jnp.zeros((field.shape[0] - NOTHING, 128), jnp.float32)
    for copy in copies:
        copy.wait()

    def rest(i, _):
        found = []
        for u in range(LIST):
            at, lane = split_index(i * LIST + u, tiles)
            block, row = place(table[list_row + at, lane])
            t, b = split_index(block, nb)
            r = dot_nt(split_rows(field, row, tiles), blocks[t, b])
            found.append((t, r[:ROWS] + r[ROWS:]))
        for t, r in found:
            total[t] += r
        return 0

    lax.fori_loop(0, lax.div(table[count_row, 0] + LIST - 1, LIST), rest, 0)


def late_first_kernel(tiles, nb, ntr, col_blocks, table, far, partial, blocks, out, field, total, fsem):
    load_far(tiles, nb, col_blocks, table, far, blocks, field, total, fsem)
    for t in range(tiles):
        v = far_product(tiles, nb, table, field, blocks, t) + partial[t] + total[t]
        out[pl.ds(t, ntr, stride=tiles), :] = v[:ntr]


def late_second_kernel(tiles, nb, ntr, col_blocks, table, far, partial, blocks, rates, depths, mix, sink,
                       out, field, total, value, fsem):
    load_far(tiles, nb, col_blocks, table, far, blocks, field, total, fsem)
    order_row = table_rows(nb, col_blocks)[0]
    per = LATE_GROUP // col_blocks
    steps = tiles // LATE_GROUP

    def products(c):
        for u in range(LATE_GROUP):
            t = table[order_row + u % col_blocks, c * per + u // col_blocks]
            value[c % 2 if isinstance(c, int) else lax.rem(c, 2), u] = (
                far_product(tiles, nb, table, field, blocks, t) + partial[t] + total[t])

    def chain(c, carry):
        carry = list(carry)
        for l in range(per):
            k = c * per + l
            for q in range(col_blocks):
                u = l * col_blocks + q
                t = table[order_row + q, k]
                v = value[c % 2 if isinstance(c, int) else lax.rem(c, 2), u]
                mixed = mix[0] * v[0:1]
                for s in range(1, ntr):
                    mixed = mixed + mix[s] * v[s:s + 1]
                wet = k < depths[:, q * 128:(q + 1) * 128]
                y = jnp.where(wet, v + rates[k, q:q + 1] * mixed + carry[q], jnp.float32(0.0))
                carry[q] = sink[...] * y
                out[pl.ds(t, ntr, stride=tiles), :] = y[:ntr]
        return tuple(carry)

    carry = tuple(jnp.zeros((ROWS, 128), jnp.float32) for _ in range(col_blocks))
    products(0)

    def step(c, carry):
        products(c)
        return chain(c - 1, carry)

    if UNROLL:
        for c in range(1, steps):
            carry = step(c, carry)
    else:
        carry = lax.fori_loop(1, steps, step, carry)
    chain(steps - 1, carry)


def in_hbm(x):
    return pltpu.with_memory_space_constraint(x, pltpu.HBM)


def exchange(rows):
    n = lax.axis_size("region")
    near = [(i, i ^ 1) for i in range(n)]
    far = [(i, (i + 1) % n if i % 2 else (i - 1) % n) for i in range(n)]
    b = lax.ppermute(rows, "region", far)
    a = lax.ppermute(rows, "region", near)
    return a, b


def exchange_split(rows):
    n = lax.axis_size("region")
    near = [(i, i ^ 1) for i in range(n)]
    far = [(i, (i + 1) % n if i % 2 else (i - 1) % n) for i in range(n)]
    b = lax.ppermute(rows, "region", far)
    half = rows.shape[0] // 2
    a = [lax.ppermute(rows[i * half:(i + 1) * half], "region", near) for i in range(2)]
    return a, b


def shards(tangent, transport, block_column, cell_order, depths, rates, coupling, sinking):
    tiles, ntr, cells = tangent.shape
    nb = block_column.shape[2]
    levels, col_blocks = cell_order.shape
    rows = ntr * tiles
    chunks = tiles // CHUNK
    planar = jnp.transpose(tangent, (1, 0, 2)).reshape(rows, cells)
    near, far = exchange(planar)

    smem = pl.BlockSpec(memory_space=pltpu.SMEM)
    vmem = pl.BlockSpec(memory_space=pltpu.VMEM)
    anyw = pl.BlockSpec(memory_space=pl.ANY)
    params = pltpu.CompilerParams(vmem_limit_bytes=VMEM_LIMIT)
    cost = pl.CostEstimate(
        flops=4 * tiles * nb * cells * cells * ntr, bytes_accessed=transport.size, transcendentals=0
    )
    none = pl.CostEstimate(flops=0, bytes_accessed=0, transcendentals=0)
    f32, i32 = jnp.float32, jnp.int32
    array = jax.ShapeDtypeStruct
    blocks_shape = pltpu.VMEM(transport.shape[1:], transport.dtype)
    pad = (ROWS - ntr) * tiles
    sems = pltpu.SemaphoreType.DMA

    picks = in_hbm(jnp.transpose(block_column, (0, 2, 1)))
    own = in_hbm(planar)
    table_shape = array((table_rows(nb, col_blocks)[2] + 8 & ~7, tiles), i32)
    regions = lax.axis_size("region")
    partial_shape = array((tiles, ROWS, cells), f32)
    picks_scratch = pltpu.VMEM((nb, tiles), i32)
    staged = pltpu.VMEM(table_shape.shape, i32)
    field = pltpu.VMEM((3 * rows + pad, cells), f32)
    far_field = pltpu.VMEM((2 * NOTHING, cells), f32)
    total = pltpu.VMEM((tiles, ROWS, cells), f32)

    blocks, partial, table = pl.pallas_call(
        functools.partial(early_first_kernel, tiles, nb, ntr, col_blocks, regions),
        out_shape=(blocks_shape, partial_shape, table_shape),
        in_specs=[anyw] * 4,
        out_specs=[vmem, vmem, smem],
        scratch_shapes=[picks_scratch, staged, field, sems, sems((2,)), sems((chunks,))],
        compiler_params=params,
        cost_estimate=none,
        name="step_one_early",
    )(picks, own, near, transport)

    middle = pl.pallas_call(
        functools.partial(late_first_kernel, tiles, nb, ntr, col_blocks),
        out_shape=array((rows, cells), f32),
        in_specs=[smem, anyw, vmem, vmem],
        out_specs=vmem,
        scratch_shapes=[far_field, total, sems((1,))],
        compiler_params=params,
        cost_estimate=cost,
        name="step_one_late",
    )(table, far, partial, blocks)

    near, far = exchange_split(middle)
    blocks, partial, table, level_rates, mix, sink = pl.pallas_call(
        functools.partial(early_second_kernel, tiles, nb, ntr, col_blocks, regions),
        out_shape=(
            blocks_shape,
            partial_shape,
            table_shape,
            array((levels, col_blocks, cells), f32),
            array((ntr, ROWS, cells), f32),
            array((ROWS, cells), f32),
        ),
        in_specs=[anyw] * 4 + [smem] + [anyw] * 4,
        out_specs=[vmem, vmem, smem, vmem, vmem, vmem],
        scratch_shapes=[
            picks_scratch,
            staged,
            field,
            pltpu.VMEM((col_blocks, levels), i32),
            pltpu.VMEM(rates.shape, f32),
            pltpu.VMEM(coupling.shape, f32),
            sems,
            sems((3,)),
            sems((3,)),
            sems((chunks,)),
        ],
        compiler_params=params,
        cost_estimate=none,
        name="step_two_early",
    )(picks, in_hbm(cell_order.T), in_hbm(rates), in_hbm(coupling), sinking, middle, *near, transport)

    result = pl.pallas_call(
        functools.partial(late_second_kernel, tiles, nb, ntr, col_blocks),
        out_shape=array((rows, cells), f32),
        in_specs=[smem, anyw] + [vmem] * 6,
        out_specs=vmem,
        scratch_shapes=[far_field, total, pltpu.VMEM((2, LATE_GROUP, ROWS, cells), f32), sems((1,))],
        compiler_params=params,
        cost_estimate=cost,
        name="step_two_late",
    )(table, far, partial, blocks, level_rates, depths.reshape(1, -1), mix, sink)
    return jnp.transpose(result.reshape(ntr, tiles, cells), (1, 0, 2))


def solution(mesh):
    in_specs = (
        P(("groups", "region"), None, None),
        P(None, "region", None, None, None),
        P(None, "region", None),
        P(None, "region"),
        P("region"),
        P(None, "region"),
        P(),
        P(),
    )
    out_specs = P(("groups", "region"), None, None)
    return jax.shard_map(shards, mesh=mesh, in_specs=in_specs, out_specs=out_specs, check_vma=False)
```

time: 49.4 us -> 46.6 us (0.943)
  local copies, waits for them, and re-layouts: 3.61 us -> 0.05 us
  starting transfers between devices: 7.86 us -> 4.75 us
  Pallas kernels: 29.1 us -> 31.1 us
  waiting for transfers between devices: 8.72 us -> 10.3 us
    ppermute x1, waiting for transfers between devices: 2.45 us -> 6.38 us  [exchange(): b = lax.ppermute(rows, 'region', far)]
    unnamed x14 -> x4, local copies, waits for them, and re-layouts: 3.57 us -> 0.01 us
    ppermute x1, starting transfers between devices: 2.87 us -> 0.06 us  [exchange(): a = lax.ppermute(rows, 'region', near)]
    ppermute x1, waiting for transfers between devices: 4.68 us -> 2.3 us  [exchange_split(): b = lax.ppermute(rows, 'region', far)]
    pallas_call x4, Pallas kernels: 29.1 us -> 31.1 us  [the longest x1 9.97 us: shards(): pl.pallas_call(functools.partial(early_second_kernel, tiles, nb, ntr, col...]
  transfers between devices with their start and end apart: 5 -> 5, of which waited for: 4 -> 4; matrix products, arithmetic and copies ran while one was open for 0% -> 0% of each run, Pallas kernels for 30% -> 41%
where the time goes in v3:
time: 46.6 us; the launch traced here: 46.2 us
  Pallas kernels  31.1 us (67%)
  waiting for transfers between devices  10.3 us (22%)
  starting transfers between devices  4.75 us (10%)
    pallas_call x1, Pallas kernels, shards(): pl.pallas_call(functools.partial(early_second_kernel, tiles, nb, ntr, col...  9.97 us
    pallas_call x1, Pallas kernels, shards(): pl.pallas_call(functools.partial(early_first_kernel, tiles, nb, ntr, col_...  9.1 us
    pallas_call x1, Pallas kernels, shards(): pl.pallas_call(functools.partial(late_second_kernel, tiles, nb, ntr, col_...  6.68 us
    ppermute x1, waiting for transfers between devices, exchange(): b = lax.ppermute(rows, 'region', far)  6.38 us
    pallas_call x1, Pallas kernels, shards(): pl.pallas_call(functools.partial(late_first_kernel, tiles, nb, ntr, col_b...  5.35 us
    ppermute x1, starting transfers between devices, exchange(): b = lax.ppermute(rows, 'region', far)  2.57 us
    ppermute x1, waiting for transfers between devices, exchange_split(): b = lax.ppermute(rows, 'region', far)  2.3 us
    ppermute x2, waiting for transfers between devices, exchange_split(): lax.ppermute(rows[i * half:(i + 1) * half], 'region', near)  1.59 us
  transfers between devices with their start and end apart: 5, of which 4 were waited for; matrix products, arithmetic and copies ran while one was open for 0% of the time, Pallas kernels for 41%

profile of v3, /device:TPU:1, one launch (start us, length us, event | category | flops | bytes accessed | tf_op | source)
XLA Modules:
  0.0 46.2 jit_solution(14522683024400613399)
XLA Ops:
  0.0 0.1 collective-permute-start
  0.1 2.6 %collective-permute-start.1 = (f32[1280,128]{1,0:T(8,128)}, f32[1280,128]{1,0:T(8,128)S(1)}, u32[]{:S(2)}, u32[]{:S(2)}) collective-permute-start(f32[1280,128]{1,0:T(8,128)} %bitcast.11), channel_id=1, source_target_pairs={{0,15},{1,2},{2,1},{3,4},{4,3},{5,6},{6,5},{7,8},{8,7},{9,10},{10,... | collective-permute-start | bytes 1966088 | tf_op jit(solution)/shard_map/ppermute | solution.py:273
  2.6 0.0 collective-permute-done.near
  2.6 9.1 %step_one_early.1 = (bf16[128,4,128,128]{3,2,1,0:T(8,128)(2,1)S(1)}, f32[128,16,128]{2,1,0:T(8,128)S(1)}, s32[24,128]{1,0:T(8,128)S(1)}) custom-call(s32[2,4,128]{2,1,0:T(4,128)} %bitcast.13, f32[1280,128]{1,0:T(8,128)} %bitcast.12, f32[1280,128]{1,0:T(8,128)S(1)} %collective-permute-done.near, bf16[2,128,4,128,128]{4,3,2,1,0:T(8,128)(2,1)} %transport.3), custom_call_target="tpu_custom_call" | custom-call | tf_op jit(solution)/shard_map/step_one_early/pallas_call | solution.py:322
  11.7 0.0 copy-start.1
  11.8 6.4 %collective-permute-done.1.far = f32[1280,128]{1,0:T(8,128)S(1)} collective-permute-done((f32[1280,128]{1,0:T(8,128)}, f32[1280,128]{1,0:T(8,128)S(1)}, u32[]{:S(2)}, u32[]{:S(2)}) %collective-permute-start.1) | collective-permute-done | bytes 655392 | tf_op jit(solution)/shard_map/ppermute | solution.py:273
  18.1 5.4 %step_one_late.1.own = f32[1280,128]{1,0:T(8,128)S(1)} custom-call(s32[24,128]{1,0:T(8,128)S(1)} %get-tuple-element.14.table, f32[1280,128]{1,0:T(8,128)S(1)} %collective-permute-done.1.far, f32[128,16,128]{2,1,0:T(8,128)S(1)} %get-tuple-element.15.partial, bf16[128,4,128,128]{3,2,1,0:T(8,128)(2,1)S(1)} %get-tuple-element.16.blocks), custom_call_target="tpu_custom_call" | custom-call | flops 335544320 | bytes 16777216 | tf_op jit(solution)/shard_map/step_one_late/pallas_call | solution.py:333
  23.5 1.6 %collective-permute-start.4 = (f32[1280,128]{1,0:T(8,128)S(1)}, f32[1280,128]{1,0:T(8,128)S(1)}, u32[]{:S(2)}, u32[]{:S(2)}) collective-permute-start(f32[1280,128]{1,0:T(8,128)S(1)} %step_one_late.1.own), channel_id=1, source_target_pairs={{0,15},{1,2},{2,1},{3,4},{4,3},{5,6},{6,5},{7,8},{8,7},{9,10},{10,... | collective-permute-start | bytes 1966088 | tf_op jit(solution)/shard_map/ppermute | solution.py:282
  25.1 0.1 collective-permute-start.2
  25.2 0.5 %collective-permute-start.3 = (f32[640,128]{1,0:T(8,128)S(1)}, f32[640,128]{1,0:T(8,128)S(1)}, u32[]{:S(2)}, u32[]{:S(2)}) collective-permute-start(f32[640,128]{1,0:T(8,128)S(1)} %get-tuple-element.23), channel_id=1, source_target_pairs={{0,1},{1,0},{2,3},{3,2},{4,5},{5,4},{6,7},{7,6},{8,9},{9,8},{10,11... | collective-permute-start | bytes 983048 | tf_op jit(solution)/shard_map/ppermute | solution.py:284
  25.7 1.1 %collective-permute-done.2.near = f32[640,128]{1,0:T(8,128)S(1)} collective-permute-done((f32[640,128]{1,0:T(8,128)S(1)}, f32[640,128]{1,0:T(8,128)S(1)}, u32[]{:S(2)}, u32[]{:S(2)}) %collective-permute-start.2) | collective-permute-done | bytes 327712 | tf_op jit(solution)/shard_map/ppermute | solution.py:284
  26.8 0.5 %collective-permute-done.3.near_end = f32[640,128]{1,0:T(8,128)S(1)} collective-permute-done((f32[640,128]{1,0:T(8,128)S(1)}, f32[640,128]{1,0:T(8,128)S(1)}, u32[]{:S(2)}, u32[]{:S(2)}) %collective-permute-start.3) | collective-permute-done | bytes 327712 | tf_op jit(solution)/shard_map/ppermute | solution.py:284
  27.3 0.0 copy-done.1
  27.3 0.0 copy-start
  27.3 10.0 %step_two_early.1 = (bf16[128,4,128,128]{3,2,1,0:T(8,128)(2,1)S(1)}, f32[128,16,128]{2,1,0:T(8,128)S(1)}, s32[24,128]{1,0:T(8,128)S(1)}, f32[32,4,128]{2,1,0:T(4...) custom-call(s32[2,4,128]{2,1,0:T(4,128)} %bitcast.14, s32[4,32]{1,0:T(4,128)} %bitcast.15, ...), custom_call_target="tpu_custom_call" | custom-call | tf_op jit(solution)/shard_map/step_two_early/pallas_call | solution.py:345
  37.2 2.3 %collective-permute-done.4.far = f32[1280,128]{1,0:T(8,128)S(1)} collective-permute-done((f32[1280,128]{1,0:T(8,128)S(1)}, f32[1280,128]{1,0:T(8,128)S(1)}, u32[]{:S(2)}, u32[]{:S(2)}) %collective-permute-start.4) | collective-permute-done | bytes 655392 | tf_op jit(solution)/shard_map/ppermute | solution.py:282
  39.5 0.0 copy-done
  39.5 6.7 %step_two_late.1 = f32[1280,128]{1,0:T(8,128)} custom-call(s32[24,128]{1,0:T(8,128)S(1)} %get-tuple-element.17.table, f32[1280,128]{1,0:T(8,128)S(1)} %collective-permute-done.4.far, f32[128,16,128]{2,1,0:T(8,128)S(1)} %get-tuple-element.18.partial, bf16[128,4,128,128]{3,2,1,0:T(8,128)(2,1)S(1)} %get-tuple-element.19.blocks, ...), custom_call_target="tpu_custom_call" | custom-call | flops 335544320 | bytes 16777216 | tf_op jit(solution)/shard_map/step_two_late/pallas_call | solution.py:374
  (1 shorter events, 0.0 us)
Async XLA Ops:
  0.0 2.6 %collective-permute-start = (f32[1280,128]{1,0:T(8,128)}, f32[1280,128]{1,0:T(8,128)S(1)}, u32[]{:S(2)}, u32[]{:S(2)}) collective-permute-start(f32[1280,128]{1,0:T(8,128)} %bitcast.10), channel_id=1, source_target_pairs={{0,1},{1,0},{2,3},{3,2},{4,5},{5,4},{6,7},{7,6},{8,9},{9,8},{10,11... | collective-permute-start | bytes 1966088 | tf_op jit(solution)/shard_map/ppermute | solution.py:274
  0.1 18.1 %collective-permute-start.1 = (f32[1280,128]{1,0:T(8,128)}, f32[1280,128]{1,0:T(8,128)S(1)}, u32[]{:S(2)}, u32[]{:S(2)}) collective-permute-start(f32[1280,128]{1,0:T(8,128)} %bitcast.11), channel_id=1, source_target_pairs={{0,15},{1,2},{2,1},{3,4},{4,3},{5,6},{6,5},{7,8},{8,7},{9,10},{10,... | collective-permute-start | bytes 1966088 | tf_op jit(solution)/shard_map/ppermute | solution.py:273
  11.7 15.5 %copy-start.1 = (f32[10]{0:T(128)S(1)}, f32[10]{0:T(128)}, u32[]{:S(2)}) copy-start(f32[10]{0:T(128)} %sinking.1) | copy-start | bytes 124
  23.5 16.0 %collective-permute-start.4 = (f32[1280,128]{1,0:T(8,128)S(1)}, f32[1280,128]{1,0:T(8,128)S(1)}, u32[]{:S(2)}, u32[]{:S(2)}) collective-permute-start(f32[1280,128]{1,0:T(8,128)S(1)} %step_one_late.1.own), channel_id=1, source_target_pairs={{0,15},{1,2},{2,1},{3,4},{4,3},{5,6},{6,5},{7,8},{8,7},{9,10},{10,... | collective-permute-start | bytes 1966088 | tf_op jit(solution)/shard_map/ppermute | solution.py:282
  25.1 1.7 %collective-permute-start.2 = (f32[640,128]{1,0:T(8,128)S(1)}, f32[640,128]{1,0:T(8,128)S(1)}, u32[]{:S(2)}, u32[]{:S(2)}) collective-permute-start(f32[640,128]{1,0:T(8,128)S(1)} %get-tuple-element.24), channel_id=1, source_target_pairs={{0,1},{1,0},{2,3},{3,2},{4,5},{5,4},{6,7},{7,6},{8,9},{9,8},{10,11... | collective-permute-start | bytes 983048 | tf_op jit(solution)/shard_map/ppermute | solution.py:284
  25.2 2.1 %collective-permute-start.3 = (f32[640,128]{1,0:T(8,128)S(1)}, f32[640,128]{1,0:T(8,128)S(1)}, u32[]{:S(2)}, u32[]{:S(2)}) collective-permute-start(f32[640,128]{1,0:T(8,128)S(1)} %get-tuple-element.23), channel_id=1, source_target_pairs={{0,1},{1,0},{2,3},{3,2},{4,5},{5,4},{6,7},{7,6},{8,9},{9,8},{10,11... | collective-permute-start | bytes 983048 | tf_op jit(solution)/shard_map/ppermute | solution.py:284
  27.3 12.3 %copy-start = (s32[512]{0:T(512)S(1)}, s32[512]{0:T(512)}, u32[]{:S(2)}) copy-start(s32[512]{0:T(512)} %param.12) | copy-start | bytes 6148

commit v4 on v3

--- a/solution.py
+++ b/solution.py
@@ -10,6 +10,7 @@
 GROUP = 16
 CHUNK = 8
 LIST = 8
+STATIC = 24
 LATE_GROUP = 16
 UNROLL = True
 DIRECT = 2
@@ -17,6 +18,16 @@
 NOTHING = 2048
 ROWS = 16
 VMEM_LIMIT = 12 * 1024 * 1024
+
+
+def far_rows(far, row, tiles):
+    ntr = far.shape[0] // tiles
+    keep = jnp.where(row < tiles, 1.0, 0.0).astype(jnp.float32)
+    x = far[pl.ds(jnp.where(row < tiles, row, 0), ntr, stride=tiles), :] * keep
+    x = jnp.concatenate([x, jnp.zeros((ROWS - ntr, 128), jnp.float32)], axis=0)
+    high = x.astype(jnp.bfloat16)
+    low = (x - high.astype(jnp.float32)).astype(jnp.bfloat16)
+    return jnp.concatenate([high, low], axis=0)
 
 
 def dot_nt(x, t):
@@ -105,7 +116,7 @@
 
     n = lax.fori_loop(0, tiles // GROUP, step, jnp.int32(0))
     table[count_row, 0] = n
-    for i in range(LIST):
+    for i in range(STATIC):
         put(n + i, NOTHING)
 
 
@@ -181,45 +192,45 @@
     xs, ts = [], []
     for m in range(DIRECT):
         b, row = place(table[nb + m, t])
-        xs.append(split_rows(field, row, tiles))
+        xs.append(far_rows(field, row, tiles))
         ts.append(blocks[t, b])
     r = dot_nt(jnp.concatenate(xs, axis=1), jnp.concatenate(ts, axis=1))
     return r[:ROWS] + r[ROWS:]
 
 
-def load_far(tiles, nb, col_blocks, table, far, blocks, field, total, fsem):
+def load_far(tiles, nb, col_blocks, table, field, blocks, total):
     order_row, list_row, count_row = table_rows(nb, col_blocks)
-    copies = copy_rows((far,), field, fsem)
     total[...] = jnp.zeros_like(total)
-    field[NOTHING:, :] = jnp.zeros((field.shape[0] - NOTHING, 128), jnp.float32)
-    for copy in copies:
-        copy.wait()
-
-    def rest(i, _):
+
+    def rest(first, size):
         found = []
-        for u in range(LIST):
-            at, lane = split_index(i * LIST + u, tiles)
+        for u in range(size):
+            at, lane = split_index(first + u, tiles)
             block, row = place(table[list_row + at, lane])
             t, b = split_index(block, nb)
-            r = dot_nt(split_rows(field, row, tiles), blocks[t, b])
+            r = dot_nt(far_rows(field, row, tiles), blocks[t, b])
             found.append((t, r[:ROWS] + r[ROWS:]))
         for t, r in found:
             total[t] += r
+
+    def more(i, _):
+        rest(STATIC + i * LIST, LIST)
         return 0
 
-    lax.fori_loop(0, lax.div(table[count_row, 0] + LIST - 1, LIST), rest, 0)
-
-
-def late_first_kernel(tiles, nb, ntr, col_blocks, table, far, partial, blocks, out, field, total, fsem):
-    load_far(tiles, nb, col_blocks, table, far, blocks, field, total, fsem)
+    lax.fori_loop(0, lax.div(jnp.maximum(table[count_row, 0] - STATIC, 0) + LIST - 1, LIST), more, 0)
+    rest(jnp.int32(0), STATIC)
+
+
+def late_first_kernel(tiles, nb, ntr, col_blocks, table, field, partial, blocks, out, total):
+    load_far(tiles, nb, col_blocks, table, field, blocks, total)
     for t in range(tiles):
         v = far_product(tiles, nb, table, field, blocks, t) + partial[t] + total[t]
         out[pl.ds(t, ntr, stride=tiles), :] = v[:ntr]
 
 
-def late_second_kernel(tiles, nb, ntr, col_blocks, table, far, partial, blocks, rates, depths, mix, sink,
-                       out, field, total, value, fsem):
-    load_far(tiles, nb, col_blocks, table, far, blocks, field, total, fsem)
+def late_second_kernel(tiles, nb, ntr, col_blocks, table, field, partial, blocks, rates, depths, mix, sink,
+                       out, total, value):
+    load_far(tiles, nb, col_blocks, table, field, blocks, total)
     order_row = table_rows(nb, col_blocks)[0]
     per = LATE_GROUP // col_blocks
     steps = tiles // LATE_GROUP
@@ -316,7 +327,6 @@
     picks_scratch = pltpu.VMEM((nb, tiles), i32)
     staged = pltpu.VMEM(table_shape.shape, i32)
     field = pltpu.VMEM((3 * rows + pad, cells), f32)
-    far_field = pltpu.VMEM((2 * NOTHING, cells), f32)
     total = pltpu.VMEM((tiles, ROWS, cells), f32)
 
     blocks, partial, table = pl.pallas_call(
@@ -333,9 +343,9 @@
     middle = pl.pallas_call(
         functools.partial(late_first_kernel, tiles, nb, ntr, col_blocks),
         out_shape=array((rows, cells), f32),
-        in_specs=[smem, anyw, vmem, vmem],
+        in_specs=[smem, vmem, vmem, vmem],
         out_specs=vmem,
-        scratch_shapes=[far_field, total, sems((1,))],
+        scratch_shapes=[total],
         compiler_params=params,
         cost_estimate=cost,
         name="step_one_late",
@@ -374,9 +384,9 @@
     result = pl.pallas_call(
         functools.partial(late_second_kernel, tiles, nb, ntr, col_blocks),
         out_shape=array((rows, cells), f32),
-        in_specs=[smem, anyw] + [vmem] * 6,
+        in_specs=[smem, vmem] + [vmem] * 6,
         out_specs=vmem,
-        scratch_shapes=[far_field, total, pltpu.VMEM((2, LATE_GROUP, ROWS, cells), f32), sems((1,))],
+        scratch_shapes=[total, pltpu.VMEM((2, LATE_GROUP, ROWS, cells), f32)],
         compiler_params=params,
         cost_estimate=cost,
         name="step_two_late",

time: 46.6 us -> 44.5 us (0.955)
  Pallas kernels: 31.1 us -> 29 us
    pallas_call x1, Pallas kernels: 6.68 us -> 5.63 us  [shards(): pl.pallas_call(functools.partial(late_second_kernel, tiles, nb, ntr, col_...]
    pallas_call x1, Pallas kernels: 5.35 us -> 4.31 us  [shards(): pl.pallas_call(functools.partial(late_first_kernel, tiles, nb, ntr, col_b...]
  transfers between devices with their start and end apart: 5 -> 5, of which waited for: 4 -> 4; matrix products, arithmetic and copies ran while one was open for 0% -> 0% of each run, Pallas kernels for 41% -> 43%
where the time goes in v4:
time: 44.5 us; the launch traced here: 44.4 us
  Pallas kernels  29 us (65%)
  waiting for transfers between devices  10.2 us (23%)
  starting transfers between devices  5 us (11%)
    pallas_call x1, Pallas kernels, shards(): pl.pallas_call(functools.partial(early_second_kernel, tiles, nb, ntr, col...  9.98 us
    pallas_call x1, Pallas kernels, shards(): pl.pallas_call(functools.partial(early_first_kernel, tiles, nb, ntr, col_...  9.09 us
    ppermute x1, waiting for transfers between devices, exchange(): b = lax.ppermute(rows, 'region', far)  6.39 us
    pallas_call x1, Pallas kernels, shards(): pl.pallas_call(functools.partial(late_second_kernel, tiles, nb, ntr, col_...  5.63 us
    pallas_call x1, Pallas kernels, shards(): pl.pallas_call(functools.partial(late_first_kernel, tiles, nb, ntr, col_b...  4.31 us
    ppermute x1, starting transfers between devices, exchange(): b = lax.ppermute(rows, 'region', far)  2.57 us
    ppermute x1, waiting for transfers between devices, exchange_split(): b = lax.ppermute(rows, 'region', far)  2.26 us
    ppermute x1, starting transfers between devices, exchange_split(): b = lax.ppermute(rows, 'region', far)  1.8 us
  transfers between devices with their start and end apart: 5, of which 4 were waited for; matrix products, arithmetic and copies ran while one was open for 0% of the time, Pallas kernels for 43%

profile of v4, /device:TPU:1, one launch (start us, length us, event | category | flops | bytes accessed | tf_op | source)
XLA Modules:
  0.0 44.4 jit_solution(16092288474664856257)
XLA Ops:
  0.0 0.1 collective-permute-start
  0.1 2.6 %collective-permute-start.1 = (f32[1280,128]{1,0:T(8,128)}, f32[1280,128]{1,0:T(8,128)S(1)}, u32[]{:S(2)}, u32[]{:S(2)}) collective-permute-start(f32[1280,128]{1,0:T(8,128)} %bitcast.11), channel_id=1, source_target_pairs={{0,15},{1,2},{2,1},{3,4},{4,3},{5,6},{6,5},{7,8},{8,7},{9,10},{10,... | collective-permute-start | bytes 1966088 | tf_op jit(solution)/shard_map/ppermute | solution.py:284
  2.6 0.0 collective-permute-done.near
  2.6 9.1 %step_one_early.1 = (bf16[128,4,128,128]{3,2,1,0:T(8,128)(2,1)S(1)}, f32[128,16,128]{2,1,0:T(8,128)S(1)}, s32[24,128]{1,0:T(8,128)S(1)}) custom-call(s32[2,4,128]{2,1,0:T(4,128)} %bitcast.13, f32[1280,128]{1,0:T(8,128)} %bitcast.12, f32[1280,128]{1,0:T(8,128)S(1)} %collective-permute-done.near, bf16[2,128,4,128,128]{4,3,2,1,0:T(8,128)(2,1)} %transport.3), custom_call_target="tpu_custom_call" | custom-call | tf_op jit(solution)/shard_map/step_one_early/pallas_call | solution.py:332
  11.7 0.0 copy-start.1
  11.7 6.4 %collective-permute-done.1.field = f32[1280,128]{1,0:T(8,128)S(1)} collective-permute-done((f32[1280,128]{1,0:T(8,128)}, f32[1280,128]{1,0:T(8,128)S(1)}, u32[]{:S(2)}, u32[]{:S(2)}) %collective-permute-start.1) | collective-permute-done | bytes 655392 | tf_op jit(solution)/shard_map/ppermute | solution.py:284
  18.1 4.3 %step_one_late.1.own = f32[1280,128]{1,0:T(8,128)S(1)} custom-call(s32[24,128]{1,0:T(8,128)S(1)} %get-tuple-element.14.table, f32[1280,128]{1,0:T(8,128)S(1)} %collective-permute-done.1.field, f32[128,16,128]{2,1,0:T(8,128)S(1)} %get-tuple-element.15.partial, bf16[128,4,128,128]{3,2,1,0:T(8,128)(2,1)S(1)} %get-tuple-element.16.blocks), custom_call_target="tpu_custom_call" | custom-call | flops 335544320 | bytes 16777216 | tf_op jit(solution)/shard_map/step_one_late/pallas_call | solution.py:343
  22.5 1.8 %collective-permute-start.4 = (f32[1280,128]{1,0:T(8,128)S(1)}, f32[1280,128]{1,0:T(8,128)S(1)}, u32[]{:S(2)}, u32[]{:S(2)}) collective-permute-start(f32[1280,128]{1,0:T(8,128)S(1)} %step_one_late.1.own), channel_id=1, source_target_pairs={{0,15},{1,2},{2,1},{3,4},{4,3},{5,6},{6,5},{7,8},{8,7},{9,10},{10,... | collective-permute-start | bytes 1966088 | tf_op jit(solution)/shard_map/ppermute | solution.py:293
  24.3 0.1 collective-permute-start.2
  24.4 0.5 %collective-permute-start.3 = (f32[640,128]{1,0:T(8,128)S(1)}, f32[640,128]{1,0:T(8,128)S(1)}, u32[]{:S(2)}, u32[]{:S(2)}) collective-permute-start(f32[640,128]{1,0:T(8,128)S(1)} %get-tuple-element.23), channel_id=1, source_target_pairs={{0,1},{1,0},{2,3},{3,2},{4,5},{5,4},{6,7},{7,6},{8,9},{9,8},{10,11... | collective-permute-start | bytes 983048 | tf_op jit(solution)/shard_map/ppermute | solution.py:295
  24.9 1.1 %collective-permute-done.2.near = f32[640,128]{1,0:T(8,128)S(1)} collective-permute-done((f32[640,128]{1,0:T(8,128)S(1)}, f32[640,128]{1,0:T(8,128)S(1)}, u32[]{:S(2)}, u32[]{:S(2)}) %collective-permute-start.2) | collective-permute-done | bytes 327712 | tf_op jit(solution)/shard_map/ppermute | solution.py:295
  26.0 0.5 %collective-permute-done.3.near_end = f32[640,128]{1,0:T(8,128)S(1)} collective-permute-done((f32[640,128]{1,0:T(8,128)S(1)}, f32[640,128]{1,0:T(8,128)S(1)}, u32[]{:S(2)}, u32[]{:S(2)}) %collective-permute-start.3) | collective-permute-done | bytes 327712 | tf_op jit(solution)/shard_map/ppermute | solution.py:295
  26.5 0.0 copy-done.1
  26.5 0.0 copy-start
  26.5 10.0 %step_two_early.1 = (bf16[128,4,128,128]{3,2,1,0:T(8,128)(2,1)S(1)}, f32[128,16,128]{2,1,0:T(8,128)S(1)}, s32[24,128]{1,0:T(8,128)S(1)}, f32[32,4,128]{2,1,0:T(4...) custom-call(s32[2,4,128]{2,1,0:T(4,128)} %bitcast.14, s32[4,32]{1,0:T(4,128)} %bitcast.15, ...), custom_call_target="tpu_custom_call" | custom-call | tf_op jit(solution)/shard_map/step_two_early/pallas_call | solution.py:355
  36.5 2.3 %collective-permute-done.4.field = f32[1280,128]{1,0:T(8,128)S(1)} collective-permute-done((f32[1280,128]{1,0:T(8,128)S(1)}, f32[1280,128]{1,0:T(8,128)S(1)}, u32[]{:S(2)}, u32[]{:S(2)}) %collective-permute-start.4) | collective-permute-done | bytes 655392 | tf_op jit(solution)/shard_map/ppermute | solution.py:293
  38.7 0.0 copy-done
  38.7 5.6 %step_two_late.1 = f32[1280,128]{1,0:T(8,128)} custom-call(s32[24,128]{1,0:T(8,128)S(1)} %get-tuple-element.17.table, f32[1280,128]{1,0:T(8,128)S(1)} %collective-permute-done.4.field, f32[128,16,128]{2,1,0:T(8,128)S(1)} %get-tuple-element.18.partial, bf16[128,4,128,128]{3,2,1,0:T(8,128)(2,1)S(1)} %get-tuple-element.19.blocks, ...), custom_call_target="tpu_custom_call" | custom-call | flops 335544320 | bytes 16777216 | tf_op jit(solution)/shard_map/step_two_late/pallas_call | solution.py:384
  (1 shorter events, 0.0 us)
Async XLA Ops:
  0.0 2.6 %collective-permute-start = (f32[1280,128]{1,0:T(8,128)}, f32[1280,128]{1,0:T(8,128)S(1)}, u32[]{:S(2)}, u32[]{:S(2)}) collective-permute-start(f32[1280,128]{1,0:T(8,128)} %bitcast.10), channel_id=1, source_target_pairs={{0,1},{1,0},{2,3},{3,2},{4,5},{5,4},{6,7},{7,6},{8,9},{9,8},{10,11... | collective-permute-start | bytes 1966088 | tf_op jit(solution)/shard_map/ppermute | solution.py:285
  0.1 18.1 %collective-permute-start.1 = (f32[1280,128]{1,0:T(8,128)}, f32[1280,128]{1,0:T(8,128)S(1)}, u32[]{:S(2)}, u32[]{:S(2)}) collective-permute-start(f32[1280,128]{1,0:T(8,128)} %bitcast.11), channel_id=1, source_target_pairs={{0,15},{1,2},{2,1},{3,4},{4,3},{5,6},{6,5},{7,8},{8,7},{9,10},{10,... | collective-permute-start | bytes 1966088 | tf_op jit(solution)/shard_map/ppermute | solution.py:284
  11.7 14.7 %copy-start.1 = (f32[10]{0:T(128)S(1)}, f32[10]{0:T(128)}, u32[]{:S(2)}) copy-start(f32[10]{0:T(128)} %sinking.1) | copy-start | bytes 124
  22.5 16.3 %collective-permute-start.4 = (f32[1280,128]{1,0:T(8,128)S(1)}, f32[1280,128]{1,0:T(8,128)S(1)}, u32[]{:S(2)}, u32[]{:S(2)}) collective-permute-start(f32[1280,128]{1,0:T(8,128)S(1)} %step_one_late.1.own), channel_id=1, source_target_pairs={{0,15},{1,2},{2,1},{3,4},{4,3},{5,6},{6,5},{7,8},{8,7},{9,10},{10,... | collective-permute-start | bytes 1966088 | tf_op jit(solution)/shard_map/ppermute | solution.py:293
  24.3 1.7 %collective-permute-start.2 = (f32[640,128]{1,0:T(8,128)S(1)}, f32[640,128]{1,0:T(8,128)S(1)}, u32[]{:S(2)}, u32[]{:S(2)}) collective-permute-start(f32[640,128]{1,0:T(8,128)S(1)} %get-tuple-element.24), channel_id=1, source_target_pairs={{0,1},{1,0},{2,3},{3,2},{4,5},{5,4},{6,7},{7,6},{8,9},{9,8},{10,11... | collective-permute-start | bytes 983048 | tf_op jit(solution)/shard_map/ppermute | solution.py:295
  24.4 2.1 %collective-permute-start.3 = (f32[640,128]{1,0:T(8,128)S(1)}, f32[640,128]{1,0:T(8,128)S(1)}, u32[]{:S(2)}, u32[]{:S(2)}) collective-permute-start(f32[640,128]{1,0:T(8,128)S(1)} %get-tuple-element.23), channel_id=1, source_target_pairs={{0,1},{1,0},{2,3},{3,2},{4,5},{5,4},{6,7},{7,6},{8,9},{9,8},{10,11... | collective-permute-start | bytes 983048 | tf_op jit(solution)/shard_map/ppermute | solution.py:295
  26.5 12.3 %copy-start = (s32[512]{0:T(512)S(1)}, s32[512]{0:T(512)}, u32[]{:S(2)}) copy-start(s32[512]{0:T(512)} %param.12) | copy-start | bytes 6148

commit v5 on v4

--- a/solution.py
+++ b/solution.py
@@ -204,12 +204,21 @@
 
     def rest(first, size):
         found = []
-        for u in range(size):
-            at, lane = split_index(first + u, tiles)
-            block, row = place(table[list_row + at, lane])
-            t, b = split_index(block, nb)
-            r = dot_nt(far_rows(field, row, tiles), blocks[t, b])
-            found.append((t, r[:ROWS] + r[ROWS:]))
+        blank = jnp.zeros((2 * ROWS, 128), jnp.bfloat16)
+        for u in range(0, size, 2):
+            where, xs, ts = [], [], []
+            for v in range(2):
+                at, lane = split_index(first + u + v, tiles)
+                block, row = place(table[list_row + at, lane])
+                t, b = split_index(block, nb)
+                where.append(t)
+                xs.append(far_rows(field, row, tiles))
+                ts.append(blocks[t, b])
+            x = jnp.concatenate([jnp.concatenate([xs[0], blank], axis=1), jnp.concatenate([blank, xs[1]], axis=1)], axis=0)
+            r = dot_nt(x, jnp.concatenate(ts, axis=1))
+            for v in range(2):
+                part = r[2 * ROWS * v:2 * ROWS * (v + 1)]
+                found.append((where[v], part[:ROWS] + part[ROWS:]))
         for t, r in found:
             total[t] += r
 

time: 44.5 us -> 44.3 us (level)
  no operation moved by 1% of the time
where the time goes in v5:
time: 44.3 us; the launch traced here: 44.2 us
  Pallas kernels  28.8 us (65%)
  waiting for transfers between devices  10.2 us (23%)
  starting transfers between devices  5.01 us (11%)
    pallas_call x1, Pallas kernels, shards(): pl.pallas_call(functools.partial(early_second_kernel, tiles, nb, ntr, col...  9.98 us
    pallas_call x1, Pallas kernels, shards(): pl.pallas_call(functools.partial(early_first_kernel, tiles, nb, ntr, col_...  9.09 us
    ppermute x1, waiting for transfers between devices, exchange(): b = lax.ppermute(rows, 'region', far)  6.38 us
    pallas_call x1, Pallas kernels, shards(): pl.pallas_call(functools.partial(late_second_kernel, tiles, nb, ntr, col_...  5.55 us
    pallas_call x1, Pallas kernels, shards(): pl.pallas_call(functools.partial(late_first_kernel, tiles, nb, ntr, col_b...  4.22 us
    ppermute x1, starting transfers between devices, exchange(): b = lax.ppermute(rows, 'region', far)  2.57 us
    ppermute x1, waiting for transfers between devices, exchange_split(): b = lax.ppermute(rows, 'region', far)  2.26 us
    ppermute x1, starting transfers between devices, exchange_split(): b = lax.ppermute(rows, 'region', far)  1.81 us
  transfers between devices with their start and end apart: 5, of which 4 were waited for; matrix products, arithmetic and copies ran while one was open for 0% of the time, Pallas kernels for 43%

profile of v5, /device:TPU:1, one launch (start us, length us, event | category | flops | bytes accessed | tf_op | source)
XLA Modules:
  0.0 44.2 jit_solution(5039312588327981260)
XLA Ops:
  0.0 0.1 collective-permute-start
  0.1 2.6 %collective-permute-start.1 = (f32[1280,128]{1,0:T(8,128)}, f32[1280,128]{1,0:T(8,128)S(1)}, u32[]{:S(2)}, u32[]{:S(2)}) collective-permute-start(f32[1280,128]{1,0:T(8,128)} %bitcast.11), channel_id=1, source_target_pairs={{0,15},{1,2},{2,1},{3,4},{4,3},{5,6},{6,5},{7,8},{8,7},{9,10},{10,... | collective-permute-start | bytes 1966088 | tf_op jit(solution)/shard_map/ppermute | solution.py:293
  2.6 0.0 collective-permute-done.near
  2.6 9.1 %step_one_early.1 = (bf16[128,4,128,128]{3,2,1,0:T(8,128)(2,1)S(1)}, f32[128,16,128]{2,1,0:T(8,128)S(1)}, s32[24,128]{1,0:T(8,128)S(1)}) custom-call(s32[2,4,128]{2,1,0:T(4,128)} %bitcast.13, f32[1280,128]{1,0:T(8,128)} %bitcast.12, f32[1280,128]{1,0:T(8,128)S(1)} %collective-permute-done.near, bf16[2,128,4,128,128]{4,3,2,1,0:T(8,128)(2,1)} %transport.3), custom_call_target="tpu_custom_call" | custom-call | tf_op jit(solution)/shard_map/step_one_early/pallas_call | solution.py:341
  11.7 0.0 copy-start.1
  11.8 6.4 %collective-permute-done.1.field = f32[1280,128]{1,0:T(8,128)S(1)} collective-permute-done((f32[1280,128]{1,0:T(8,128)}, f32[1280,128]{1,0:T(8,128)S(1)}, u32[]{:S(2)}, u32[]{:S(2)}) %collective-permute-start.1) | collective-permute-done | bytes 655392 | tf_op jit(solution)/shard_map/ppermute | solution.py:293
  18.1 4.2 %step_one_late.1.own = f32[1280,128]{1,0:T(8,128)S(1)} custom-call(s32[24,128]{1,0:T(8,128)S(1)} %get-tuple-element.14.table, f32[1280,128]{1,0:T(8,128)S(1)} %collective-permute-done.1.field, f32[128,16,128]{2,1,0:T(8,128)S(1)} %get-tuple-element.15.partial, bf16[128,4,128,128]{3,2,1,0:T(8,128)(2,1)S(1)} %get-tuple-element.16.blocks), custom_call_target="tpu_custom_call" | custom-call | flops 335544320 | bytes 16777216 | tf_op jit(solution)/shard_map/step_one_late/pallas_call | solution.py:352
  22.4 1.8 %collective-permute-start.4 = (f32[1280,128]{1,0:T(8,128)S(1)}, f32[1280,128]{1,0:T(8,128)S(1)}, u32[]{:S(2)}, u32[]{:S(2)}) collective-permute-start(f32[1280,128]{1,0:T(8,128)S(1)} %step_one_late.1.own), channel_id=1, source_target_pairs={{0,15},{1,2},{2,1},{3,4},{4,3},{5,6},{6,5},{7,8},{8,7},{9,10},{10,... | collective-permute-start | bytes 1966088 | tf_op jit(solution)/shard_map/ppermute | solution.py:302
  24.2 0.1 collective-permute-start.2
  24.3 0.5 %collective-permute-start.3 = (f32[640,128]{1,0:T(8,128)S(1)}, f32[640,128]{1,0:T(8,128)S(1)}, u32[]{:S(2)}, u32[]{:S(2)}) collective-permute-start(f32[640,128]{1,0:T(8,128)S(1)} %get-tuple-element.23), channel_id=1, source_target_pairs={{0,1},{1,0},{2,3},{3,2},{4,5},{5,4},{6,7},{7,6},{8,9},{9,8},{10,11... | collective-permute-start | bytes 983048 | tf_op jit(solution)/shard_map/ppermute | solution.py:304
  24.8 1.1 %collective-permute-done.2.near = f32[640,128]{1,0:T(8,128)S(1)} collective-permute-done((f32[640,128]{1,0:T(8,128)S(1)}, f32[640,128]{1,0:T(8,128)S(1)}, u32[]{:S(2)}, u32[]{:S(2)}) %collective-permute-start.2) | collective-permute-done | bytes 327712 | tf_op jit(solution)/shard_map/ppermute | solution.py:304
  25.9 0.5 %collective-permute-done.3.near_end = f32[640,128]{1,0:T(8,128)S(1)} collective-permute-done((f32[640,128]{1,0:T(8,128)S(1)}, f32[640,128]{1,0:T(8,128)S(1)}, u32[]{:S(2)}, u32[]{:S(2)}) %collective-permute-start.3) | collective-permute-done | bytes 327712 | tf_op jit(solution)/shard_map/ppermute | solution.py:304
  26.4 0.0 copy-done.1
  26.4 0.0 copy-start
  26.4 10.0 %step_two_early.1 = (bf16[128,4,128,128]{3,2,1,0:T(8,128)(2,1)S(1)}, f32[128,16,128]{2,1,0:T(8,128)S(1)}, s32[24,128]{1,0:T(8,128)S(1)}, f32[32,4,128]{2,1,0:T(4...) custom-call(s32[2,4,128]{2,1,0:T(4,128)} %bitcast.14, s32[4,32]{1,0:T(4,128)} %bitcast.15, ...), custom_call_target="tpu_custom_call" | custom-call | tf_op jit(solution)/shard_map/step_two_early/pallas_call | solution.py:364
  36.4 2.3 %collective-permute-done.4.field = f32[1280,128]{1,0:T(8,128)S(1)} collective-permute-done((f32[1280,128]{1,0:T(8,128)S(1)}, f32[1280,128]{1,0:T(8,128)S(1)}, u32[]{:S(2)}, u32[]{:S(2)}) %collective-permute-start.4) | collective-permute-done | bytes 655392 | tf_op jit(solution)/shard_map/ppermute | solution.py:302
  38.6 0.0 copy-done
  38.6 5.5 %step_two_late.1 = f32[1280,128]{1,0:T(8,128)} custom-call(s32[24,128]{1,0:T(8,128)S(1)} %get-tuple-element.17.table, f32[1280,128]{1,0:T(8,128)S(1)} %collective-permute-done.4.field, f32[128,16,128]{2,1,0:T(8,128)S(1)} %get-tuple-element.18.partial, bf16[128,4,128,128]{3,2,1,0:T(8,128)(2,1)S(1)} %get-tuple-element.19.blocks, ...), custom_call_target="tpu_custom_call" | custom-call | flops 335544320 | bytes 16777216 | tf_op jit(solution)/shard_map/step_two_late/pallas_call | solution.py:393
  (1 shorter events, 0.0 us)
Async XLA Ops:
  0.0 2.6 %collective-permute-start = (f32[1280,128]{1,0:T(8,128)}, f32[1280,128]{1,0:T(8,128)S(1)}, u32[]{:S(2)}, u32[]{:S(2)}) collective-permute-start(f32[1280,128]{1,0:T(8,128)} %bitcast.10), channel_id=1, source_target_pairs={{0,1},{1,0},{2,3},{3,2},{4,5},{5,4},{6,7},{7,6},{8,9},{9,8},{10,11... | collective-permute-start | bytes 1966088 | tf_op jit(solution)/shard_map/ppermute | solution.py:294
  0.1 18.1 %collective-permute-start.1 = (f32[1280,128]{1,0:T(8,128)}, f32[1280,128]{1,0:T(8,128)S(1)}, u32[]{:S(2)}, u32[]{:S(2)}) collective-permute-start(f32[1280,128]{1,0:T(8,128)} %bitcast.11), channel_id=1, source_target_pairs={{0,15},{1,2},{2,1},{3,4},{4,3},{5,6},{6,5},{7,8},{8,7},{9,10},{10,... | collective-permute-start | bytes 1966088 | tf_op jit(solution)/shard_map/ppermute | solution.py:293
  11.7 14.6 %copy-start.1 = (f32[10]{0:T(128)S(1)}, f32[10]{0:T(128)}, u32[]{:S(2)}) copy-start(f32[10]{0:T(128)} %sinking.1) | copy-start | bytes 124
  22.4 16.3 %collective-permute-start.4 = (f32[1280,128]{1,0:T(8,128)S(1)}, f32[1280,128]{1,0:T(8,128)S(1)}, u32[]{:S(2)}, u32[]{:S(2)}) collective-permute-start(f32[1280,128]{1,0:T(8,128)S(1)} %step_one_late.1.own), channel_id=1, source_target_pairs={{0,15},{1,2},{2,1},{3,4},{4,3},{5,6},{6,5},{7,8},{8,7},{9,10},{10,... | collective-permute-start | bytes 1966088 | tf_op jit(solution)/shard_map/ppermute | solution.py:302
  24.2 1.7 %collective-permute-start.2 = (f32[640,128]{1,0:T(8,128)S(1)}, f32[640,128]{1,0:T(8,128)S(1)}, u32[]{:S(2)}, u32[]{:S(2)}) collective-permute-start(f32[640,128]{1,0:T(8,128)S(1)} %get-tuple-element.24), channel_id=1, source_target_pairs={{0,1},{1,0},{2,3},{3,2},{4,5},{5,4},{6,7},{7,6},{8,9},{9,8},{10,11... | collective-permute-start | bytes 983048 | tf_op jit(solution)/shard_map/ppermute | solution.py:304
  24.3 2.1 %collective-permute-start.3 = (f32[640,128]{1,0:T(8,128)S(1)}, f32[640,128]{1,0:T(8,128)S(1)}, u32[]{:S(2)}, u32[]{:S(2)}) collective-permute-start(f32[640,128]{1,0:T(8,128)S(1)} %get-tuple-element.23), channel_id=1, source_target_pairs={{0,1},{1,0},{2,3},{3,2},{4,5},{5,4},{6,7},{7,6},{8,9},{9,8},{10,11... | collective-permute-start | bytes 983048 | tf_op jit(solution)/shard_map/ppermute | solution.py:304
  26.4 12.2 %copy-start = (s32[512]{0:T(512)S(1)}, s32[512]{0:T(512)}, u32[]{:S(2)}) copy-start(s32[512]{0:T(512)} %param.12) | copy-start | bytes 6148

commit v6 on v5

--- a/solution.py
+++ b/solution.py
@@ -7,7 +7,7 @@
 from jax.experimental.pallas import tpu as pltpu
 from jax.sharding import PartitionSpec as P
 
-GROUP = 16
+GROUP = 8
 CHUNK = 8
 LIST = 8
 STATIC = 24

time: 44.3 us -> 45.1 us (1.018)
  Pallas kernels: 28.8 us -> 30.4 us
  waiting for transfers between devices: 10.2 us -> 9.48 us
    pallas_call x1, Pallas kernels: 9.09 us -> 9.86 us  [shards(): pl.pallas_call(functools.partial(early_first_kernel, tiles, nb, ntr, col_...]
    ppermute x1, waiting for transfers between devices: 6.38 us -> 5.61 us  [exchange(): b = lax.ppermute(rows, 'region', far)]
    pallas_call x1, Pallas kernels: 9.98 us -> 10.7 us  [shards(): pl.pallas_call(functools.partial(early_second_kernel, tiles, nb, ntr, col...]
  transfers between devices with their start and end apart: 5 -> 5, of which waited for: 4 -> 4; matrix products, arithmetic and copies ran while one was open for 0% -> 0% of each run, Pallas kernels for 43% -> 46%
where the time goes in v6:
time: 45.1 us; the launch traced here: 45 us
  Pallas kernels  30.4 us (67%)
  waiting for transfers between devices  9.48 us (21%)
  starting transfers between devices  5.01 us (11%)
    pallas_call x1, Pallas kernels, shards(): pl.pallas_call(functools.partial(early_second_kernel, tiles, nb, ntr, col...  10.7 us
    pallas_call x1, Pallas kernels, shards(): pl.pallas_call(functools.partial(early_first_kernel, tiles, nb, ntr, col_...  9.86 us
    ppermute x1, waiting for transfers between devices, exchange(): b = lax.ppermute(rows, 'region', far)  5.61 us
    pallas_call x1, Pallas kernels, shards(): pl.pallas_call(functools.partial(late_second_kernel, tiles, nb, ntr, col_...  5.54 us
    pallas_call x1, Pallas kernels, shards(): pl.pallas_call(functools.partial(late_first_kernel, tiles, nb, ntr, col_b...  4.2 us
    ppermute x1, starting transfers between devices, exchange(): b = lax.ppermute(rows, 'region', far)  2.57 us
    ppermute x1, waiting for transfers between devices, exchange_split(): b = lax.ppermute(rows, 'region', far)  2.28 us
    ppermute x1, starting transfers between devices, exchange_split(): b = lax.ppermute(rows, 'region', far)  1.81 us
  transfers between devices with their start and end apart: 5, of which 4 were waited for; matrix products, arithmetic and copies ran while one was open for 0% of the time, Pallas kernels for 46%

profile of v6, /device:TPU:1, one launch (start us, length us, event | category | flops | bytes accessed | tf_op | source)
XLA Modules:
  0.0 45.0 jit_solution(11357637962968012132)
XLA Ops:
  0.0 0.1 collective-permute-start
  0.1 2.6 %collective-permute-start.1 = (f32[1280,128]{1,0:T(8,128)}, f32[1280,128]{1,0:T(8,128)S(1)}, u32[]{:S(2)}, u32[]{:S(2)}) collective-permute-start(f32[1280,128]{1,0:T(8,128)} %bitcast.11), channel_id=1, source_target_pairs={{0,15},{1,2},{2,1},{3,4},{4,3},{5,6},{6,5},{7,8},{8,7},{9,10},{10,... | collective-permute-start | bytes 1966088 | tf_op jit(solution)/shard_map/ppermute | solution.py:293
  2.6 0.0 collective-permute-done.near
  2.6 9.9 %step_one_early.1 = (bf16[128,4,128,128]{3,2,1,0:T(8,128)(2,1)S(1)}, f32[128,16,128]{2,1,0:T(8,128)S(1)}, s32[24,128]{1,0:T(8,128)S(1)}) custom-call(s32[2,4,128]{2,1,0:T(4,128)} %bitcast.13, f32[1280,128]{1,0:T(8,128)} %bitcast.12, f32[1280,128]{1,0:T(8,128)S(1)} %collective-permute-done.near, bf16[2,128,4,128,128]{4,3,2,1,0:T(8,128)(2,1)} %transport.3), custom_call_target="tpu_custom_call" | custom-call | tf_op jit(solution)/shard_map/step_one_early/pallas_call | solution.py:341
  12.5 0.0 copy-start.1
  12.5 5.6 %collective-permute-done.1.field = f32[1280,128]{1,0:T(8,128)S(1)} collective-permute-done((f32[1280,128]{1,0:T(8,128)}, f32[1280,128]{1,0:T(8,128)S(1)}, u32[]{:S(2)}, u32[]{:S(2)}) %collective-permute-start.1) | collective-permute-done | bytes 655392 | tf_op jit(solution)/shard_map/ppermute | solution.py:293
  18.1 4.2 %step_one_late.1.own = f32[1280,128]{1,0:T(8,128)S(1)} custom-call(s32[24,128]{1,0:T(8,128)S(1)} %get-tuple-element.14.table, f32[1280,128]{1,0:T(8,128)S(1)} %collective-permute-done.1.field, f32[128,16,128]{2,1,0:T(8,128)S(1)} %get-tuple-element.15.partial, bf16[128,4,128,128]{3,2,1,0:T(8,128)(2,1)S(1)} %get-tuple-element.16.blocks), custom_call_target="tpu_custom_call" | custom-call | flops 335544320 | bytes 16777216 | tf_op jit(solution)/shard_map/step_one_late/pallas_call | solution.py:352
  22.3 1.8 %collective-permute-start.4 = (f32[1280,128]{1,0:T(8,128)S(1)}, f32[1280,128]{1,0:T(8,128)S(1)}, u32[]{:S(2)}, u32[]{:S(2)}) collective-permute-start(f32[1280,128]{1,0:T(8,128)S(1)} %step_one_late.1.own), channel_id=1, source_target_pairs={{0,15},{1,2},{2,1},{3,4},{4,3},{5,6},{6,5},{7,8},{8,7},{9,10},{10,... | collective-permute-start | bytes 1966088 | tf_op jit(solution)/shard_map/ppermute | solution.py:302
  24.2 0.1 collective-permute-start.2
  24.3 0.5 %collective-permute-start.3 = (f32[640,128]{1,0:T(8,128)S(1)}, f32[640,128]{1,0:T(8,128)S(1)}, u32[]{:S(2)}, u32[]{:S(2)}) collective-permute-start(f32[640,128]{1,0:T(8,128)S(1)} %get-tuple-element.23), channel_id=1, source_target_pairs={{0,1},{1,0},{2,3},{3,2},{4,5},{5,4},{6,7},{7,6},{8,9},{9,8},{10,11... | collective-permute-start | bytes 983048 | tf_op jit(solution)/shard_map/ppermute | solution.py:304
  24.8 1.1 %collective-permute-done.2.near = f32[640,128]{1,0:T(8,128)S(1)} collective-permute-done((f32[640,128]{1,0:T(8,128)S(1)}, f32[640,128]{1,0:T(8,128)S(1)}, u32[]{:S(2)}, u32[]{:S(2)}) %collective-permute-start.2) | collective-permute-done | bytes 327712 | tf_op jit(solution)/shard_map/ppermute | solution.py:304
  25.9 0.5 %collective-permute-done.3.near_end = f32[640,128]{1,0:T(8,128)S(1)} collective-permute-done((f32[640,128]{1,0:T(8,128)S(1)}, f32[640,128]{1,0:T(8,128)S(1)}, u32[]{:S(2)}, u32[]{:S(2)}) %collective-permute-start.3) | collective-permute-done | bytes 327712 | tf_op jit(solution)/shard_map/ppermute | solution.py:304
  26.4 0.0 copy-done.1
  26.4 0.0 copy-start
  26.4 10.7 %step_two_early.1 = (bf16[128,4,128,128]{3,2,1,0:T(8,128)(2,1)S(1)}, f32[128,16,128]{2,1,0:T(8,128)S(1)}, s32[24,128]{1,0:T(8,128)S(1)}, f32[32,4,128]{2,1,0:T(4...) custom-call(s32[2,4,128]{2,1,0:T(4,128)} %bitcast.14, s32[4,32]{1,0:T(4,128)} %bitcast.15, ...), custom_call_target="tpu_custom_call" | custom-call | tf_op jit(solution)/shard_map/step_two_early/pallas_call | solution.py:364
  37.1 2.3 %collective-permute-done.4.field = f32[1280,128]{1,0:T(8,128)S(1)} collective-permute-done((f32[1280,128]{1,0:T(8,128)S(1)}, f32[1280,128]{1,0:T(8,128)S(1)}, u32[]{:S(2)}, u32[]{:S(2)}) %collective-permute-start.4) | collective-permute-done | bytes 655392 | tf_op jit(solution)/shard_map/ppermute | solution.py:302
  39.4 0.0 copy-done
  39.4 5.5 %step_two_late.1 = f32[1280,128]{1,0:T(8,128)} custom-call(s32[24,128]{1,0:T(8,128)S(1)} %get-tuple-element.17.table, f32[1280,128]{1,0:T(8,128)S(1)} %collective-permute-done.4.field, f32[128,16,128]{2,1,0:T(8,128)S(1)} %get-tuple-element.18.partial, bf16[128,4,128,128]{3,2,1,0:T(8,128)(2,1)S(1)} %get-tuple-element.19.blocks, ...), custom_call_target="tpu_custom_call" | custom-call | flops 335544320 | bytes 16777216 | tf_op jit(solution)/shard_map/step_two_late/pallas_call | solution.py:393
  (1 shorter events, 0.0 us)
Async XLA Ops:
  0.0 2.6 %collective-permute-start = (f32[1280,128]{1,0:T(8,128)}, f32[1280,128]{1,0:T(8,128)S(1)}, u32[]{:S(2)}, u32[]{:S(2)}) collective-permute-start(f32[1280,128]{1,0:T(8,128)} %bitcast.10), channel_id=1, source_target_pairs={{0,1},{1,0},{2,3},{3,2},{4,5},{5,4},{6,7},{7,6},{8,9},{9,8},{10,11... | collective-permute-start | bytes 1966088 | tf_op jit(solution)/shard_map/ppermute | solution.py:294
  0.1 18.1 %collective-permute-start.1 = (f32[1280,128]{1,0:T(8,128)}, f32[1280,128]{1,0:T(8,128)S(1)}, u32[]{:S(2)}, u32[]{:S(2)}) collective-permute-start(f32[1280,128]{1,0:T(8,128)} %bitcast.11), channel_id=1, source_target_pairs={{0,15},{1,2},{2,1},{3,4},{4,3},{5,6},{6,5},{7,8},{8,7},{9,10},{10,... | collective-permute-start | bytes 1966088 | tf_op jit(solution)/shard_map/ppermute | solution.py:293
  12.5 13.9 %copy-start.1 = (f32[10]{0:T(128)S(1)}, f32[10]{0:T(128)}, u32[]{:S(2)}) copy-start(f32[10]{0:T(128)} %sinking.1) | copy-start | bytes 124
  22.3 17.1 %collective-permute-start.4 = (f32[1280,128]{1,0:T(8,128)S(1)}, f32[1280,128]{1,0:T(8,128)S(1)}, u32[]{:S(2)}, u32[]{:S(2)}) collective-permute-start(f32[1280,128]{1,0:T(8,128)S(1)} %step_one_late.1.own), channel_id=1, source_target_pairs={{0,15},{1,2},{2,1},{3,4},{4,3},{5,6},{6,5},{7,8},{8,7},{9,10},{10,... | collective-permute-start | bytes 1966088 | tf_op jit(solution)/shard_map/ppermute | solution.py:302
  24.2 1.7 %collective-permute-start.2 = (f32[640,128]{1,0:T(8,128)S(1)}, f32[640,128]{1,0:T(8,128)S(1)}, u32[]{:S(2)}, u32[]{:S(2)}) collective-permute-start(f32[640,128]{1,0:T(8,128)S(1)} %get-tuple-element.24), channel_id=1, source_target_pairs={{0,1},{1,0},{2,3},{3,2},{4,5},{5,4},{6,7},{7,6},{8,9},{9,8},{10,11... | collective-permute-start | bytes 983048 | tf_op jit(solution)/shard_map/ppermute | solution.py:304
  24.3 2.1 %collective-permute-start.3 = (f32[640,128]{1,0:T(8,128)S(1)}, f32[640,128]{1,0:T(8,128)S(1)}, u32[]{:S(2)}, u32[]{:S(2)}) collective-permute-start(f32[640,128]{1,0:T(8,128)S(1)} %get-tuple-element.23), channel_id=1, source_target_pairs={{0,1},{1,0},{2,3},{3,2},{4,5},{5,4},{6,7},{7,6},{8,9},{9,8},{10,11... | collective-permute-start | bytes 983048 | tf_op jit(solution)/shard_map/ppermute | solution.py:304
  26.4 13.0 %copy-start = (s32[512]{0:T(512)S(1)}, s32[512]{0:T(512)}, u32[]{:S(2)}) copy-start(s32[512]{0:T(512)} %param.12) | copy-start | bytes 6148
